TPU v7x, 32 devices: a whole 2x2x4 slice. The times are simulated.
32 devices in a mesh: dp: 4 (over z), fsdp: 8 (over y, x, core).
Axes of the slice: x: 2, y: 2, z: 4, core: 2. Of those that a mesh axis runs over, the one named last changes fastest.
Arguments:
- tokens: bfloat16 [32768, 768], P(('dp', 'fsdp')), may hold values from -6 to 6
- first_values: bfloat16 [32768, 384], P(('dp', 'fsdp')), may hold values from -6 to 6
- cotangent: bfloat16 [32768, 768], P(('dp', 'fsdp')), may hold values from -6 to 6
- lengths: int32 [32, 2], P(('dp', 'fsdp')), may hold values from 0 to 1024, as said below
- vectors: float32 [8832], P('fsdp'), may hold values from -1 to 1.5
- w_qkv: bfloat16 [768, 1920], P(('dp', 'fsdp')), may hold values from -0.21875 to 0.21875
- w_out: bfloat16 [768, 768], P(('dp', 'fsdp')), may hold values from -1.75 to 1.75
- w_up: bfloat16 [768, 3072], P(('dp', 'fsdp')), may hold values from -0.21875 to 0.21875
- w_down: bfloat16 [3072, 768], P(('dp', 'fsdp')), may hold values from -0.109375 to 0.109375
Outputs:
- output: bfloat16 [32768, 768], P(('dp', 'fsdp'))
- grad_tokens: bfloat16 [32768, 768], P(('dp', 'fsdp'))
- grad_first_values: bfloat16 [32768, 384], P(('dp', 'fsdp'))
- grad_vectors: float32 [8832], P('fsdp')
- grad_qkv: float32 [768, 1920], P(('dp', 'fsdp'))
- grad_out: float32 [768, 768], P(('dp', 'fsdp'))
- grad_up: float32 [768, 3072], P(('dp', 'fsdp'))
- grad_down: float32 [3072, 768], P(('dp', 'fsdp'))
Inputs may be any that keep to these rules, and one draw needn't show every extreme that they name: `lengths`: each row is either (1024, 0) or (512, 512); the first row is the former and the last row the latter.
All inputs are finite; a program needn't handle non-finite values.
Results may differ from a plain program's by a relative error of at most 0.012.
Values may be sent and summed in bfloat16 or wider, within the bound.
No kernel may reach another device: no remote copies, remote signals or barrier semaphores. Data moves between devices by JAX's collectives and lax.ppermute only.
A program may use at most 320 MiB of HBM per device.

v0:
```python
import math

import jax
import jax.numpy as jnp
from jax import lax
from jax.sharding import PartitionSpec as P

D = 768
HD = 64
FF = 3072
VD = 384


EPSILON = 1e-05


def norm_rows(v, gain, shift):
    center = v - jnp.mean(v, axis=-1, keepdims=True)
    spread = jnp.mean(center * center, axis=-1, keepdims=True)
    return center * lax.rsqrt(spread + EPSILON) * gain + shift


def gelu_tanh(v):
    return jax.nn.gelu(v, approximate=True)


def left_dot(left, right):
    return lax.dot_general(
        left, right, (((0,), (0,)), ((), ())), preferred_element_type=jnp.float32
    )


def right_dot(left, right):
    return lax.dot_general(
        left, right, (((1,), (1,)), ((), ())), preferred_element_type=jnp.float32
    )


def split_vector(whole):
    widths = (D, D, D, VD, D, D, D, FF, D)
    pieces = []
    offset = 0
    for width in widths:
        pieces.append(whole[offset : offset + width])
        offset = offset + width
    return pieces


def visible(position, doc_ids, start, block):
    part_pos = lax.dynamic_slice_in_dim(position, start, block, 0)
    part_doc = lax.dynamic_slice_in_dim(doc_ids, start, block, 0)
    return (part_pos[:, None] >= position[None, :]) & (part_doc[:, None] == doc_ids[None, :])


def block_scores(part_query, keys, allowed, scale):
    scores = (
        jnp.einsum("qhd,khd->hqk", part_query, keys, preferred_element_type=jnp.float32) * scale
    )
    return jnp.where(allowed[None], scores, -1e30)


def attend_forward(query, keys, values, doc_ids, scale):
    rows = query.shape[0]
    block = min(512, rows)
    position = jnp.arange(rows, dtype=jnp.int32)

    def one_block(index):
        start = index * block
        part_query = lax.dynamic_slice_in_dim(query, start, block, 0)
        scores = block_scores(part_query, keys, visible(position, doc_ids, start, block), scale)
        peak = jnp.max(scores, axis=-1, keepdims=True)
        weights = jnp.exp(scores - peak)
        denom = jnp.sum(weights, axis=-1, keepdims=True)
        probs = (weights / denom).astype(jnp.bfloat16)
        mixed = jnp.einsum("hqk,khd->qhd", probs, values, preferred_element_type=jnp.float32)
        return (mixed, peak + jnp.log(denom))

    mixed, logsum = lax.map(one_block, jnp.arange(rows // block, dtype=jnp.int32))
    return (mixed.reshape(rows, -1), logsum)


def attend_backward(query, keys, values, grad_mixed, logsum, doc_ids, scale):
    rows = query.shape[0]
    block = min(512, rows)
    position = jnp.arange(rows, dtype=jnp.int32)

    def one_block(carry, index):
        grad_keys, grad_values = carry
        start = index * block
        part_query = lax.dynamic_slice_in_dim(query, start, block, 0)
        part_grad = lax.dynamic_slice_in_dim(grad_mixed, start, block, 0)
        part_log = lax.dynamic_index_in_dim(logsum, index, 0, keepdims=False)
        scores = block_scores(part_query, keys, visible(position, doc_ids, start, block), scale)
        probs = jnp.exp(scores - part_log)
        grad_values = grad_values + jnp.einsum(
            "hqk,qhd->khd",
            probs.astype(jnp.bfloat16),
            part_grad,
            preferred_element_type=jnp.float32,
        )
        grad_probs = jnp.einsum(
            "qhd,khd->hqk", part_grad, values, preferred_element_type=jnp.float32
        )
        inner = jnp.sum(grad_probs * probs, axis=-1, keepdims=True)
        grad_scores = (probs * (grad_probs - inner)).astype(jnp.bfloat16)
        grad_query = (
            jnp.einsum("hqk,khd->qhd", grad_scores, keys, preferred_element_type=jnp.float32)
            * scale
        )
        grad_keys = (
            grad_keys
            + jnp.einsum(
                "hqk,qhd->khd", grad_scores, part_query, preferred_element_type=jnp.float32
            )
            * scale
        )
        return ((grad_keys, grad_values), grad_query)

    empty = jnp.zeros(keys.shape, jnp.float32)
    (grad_keys, grad_values), grad_query = lax.scan(
        one_block, (empty, empty), jnp.arange(rows // block, dtype=jnp.int32)
    )
    return (
        grad_query.reshape(rows, -1),
        grad_keys.reshape(rows, -1),
        grad_values.reshape(rows, -1),
    )


def local(tokens, first_values, cotangent, lengths, vectors, w_qkv, w_out, w_up, w_down):
    rows = tokens.shape[0]
    width = tokens.shape[1]
    fresh_width = first_values.shape[1]
    heads = width // HD
    scale = 1.0 / math.sqrt(HD)
    whole_vector = lax.all_gather(vectors, "fsdp", axis=0, tiled=True)
    (
        gain_one,
        shift_one,
        bias_query,
        bias_value,
        bias_out,
        gain_two,
        shift_two,
        bias_up,
        bias_down,
    ) = split_vector(whole_vector)
    full_qkv, full_out, full_up, full_down = (
        lax.all_gather(w_qkv, ("dp", "fsdp"), axis=0, tiled=True),
        lax.all_gather(w_out, ("dp", "fsdp"), axis=0, tiled=True),
        lax.all_gather(w_up, ("dp", "fsdp"), axis=0, tiled=True),
        lax.all_gather(w_down, ("dp", "fsdp"), axis=0, tiled=True),
    )
    position = jnp.arange(rows, dtype=jnp.int32)
    doc_ids = (position >= lengths[0, 0]).astype(jnp.int32)
    inputs = tokens.astype(jnp.float32)
    normed_one, pull_one = jax.vjp(norm_rows, inputs, gain_one, shift_one)
    act_one = normed_one.astype(jnp.bfloat16)
    mixed = jnp.dot(act_one, full_qkv, preferred_element_type=jnp.float32)
    query = (mixed[:, 0:width] + bias_query).astype(jnp.bfloat16).reshape(rows, heads, HD)
    keys = mixed[:, width : 2 * width].astype(jnp.bfloat16).reshape(rows, heads, HD)
    fresh = (mixed[:, 2 * width :] + bias_value).astype(jnp.bfloat16)
    values = jnp.concatenate([fresh, first_values], axis=1).reshape(rows, heads, HD)
    attended, logsum = attend_forward(query, keys, values, doc_ids, scale)
    attended = attended.astype(jnp.bfloat16)
    residual = inputs + (jnp.dot(attended, full_out, preferred_element_type=jnp.float32) + bias_out)
    normed_two, pull_two = jax.vjp(norm_rows, residual, gain_two, shift_two)
    act_two = normed_two.astype(jnp.bfloat16)
    before = jnp.dot(act_two, full_up, preferred_element_type=jnp.float32) + bias_up
    after, pull_gelu = jax.vjp(gelu_tanh, before)
    hidden = after.astype(jnp.bfloat16)
    output = (
        residual + jnp.dot(hidden, full_down, preferred_element_type=jnp.float32) + bias_down
    ).astype(jnp.bfloat16)
    back_qkv, back_out, back_up, back_down = (
        lax.all_gather(w_qkv, ("dp", "fsdp"), axis=0, tiled=True),
        lax.all_gather(w_out, ("dp", "fsdp"), axis=0, tiled=True),
        lax.all_gather(w_up, ("dp", "fsdp"), axis=0, tiled=True),
        lax.all_gather(w_down, ("dp", "fsdp"), axis=0, tiled=True),
    )
    cot_float = cotangent.astype(jnp.float32)
    grad_down = left_dot(hidden, cotangent)
    grad_bias_down = jnp.sum(cot_float, axis=0)
    grad_hidden = right_dot(cotangent, back_down)
    grad_before = pull_gelu(grad_hidden)[0].astype(jnp.bfloat16)
    grad_up = left_dot(act_two, grad_before)
    grad_bias_up = jnp.sum(grad_before.astype(jnp.float32), axis=0)
    grad_act_two = right_dot(grad_before, back_up)
    grad_resid_norm, grad_gain_two, grad_shift_two = pull_two(grad_act_two)
    grad_residual = cot_float + grad_resid_norm
    grad_proj = grad_residual.astype(jnp.bfloat16)
    grad_out = left_dot(attended, grad_proj)
    grad_bias_out = jnp.sum(grad_proj.astype(jnp.float32), axis=0)
    grad_attended = right_dot(grad_proj, back_out).astype(jnp.bfloat16).reshape(rows, heads, HD)
    grad_query, grad_keys, grad_values = attend_backward(
        query, keys, values, grad_attended, logsum, doc_ids, scale
    )
    grad_query = grad_query.astype(jnp.bfloat16)
    grad_keys = grad_keys.astype(jnp.bfloat16)
    grad_fresh = grad_values[:, 0:fresh_width].astype(jnp.bfloat16)
    grad_first = grad_values[:, fresh_width:].astype(jnp.bfloat16)
    grad_mixed = jnp.concatenate([grad_query, grad_keys, grad_fresh], axis=1)
    grad_qkv = left_dot(act_one, grad_mixed)
    grad_bias_query = jnp.sum(grad_query.astype(jnp.float32), axis=0)
    grad_bias_value = jnp.sum(grad_fresh.astype(jnp.float32), axis=0)
    grad_act_one = right_dot(grad_mixed, back_qkv)
    grad_in_norm, grad_gain_one, grad_shift_one = pull_one(grad_act_one)
    grad_tokens = (grad_residual + grad_in_norm).astype(jnp.bfloat16)
    grad_vector = jnp.concatenate(
        [
            grad_gain_one,
            grad_shift_one,
            grad_bias_query,
            grad_bias_value,
            grad_bias_out,
            grad_gain_two,
            grad_shift_two,
            grad_bias_up,
            grad_bias_down,
        ]
    )
    summed_vector = lax.psum(grad_vector, ("dp", "fsdp"))
    piece = vectors.shape[0]
    grad_vectors = lax.dynamic_slice_in_dim(summed_vector, lax.axis_index("fsdp") * piece, piece, 0)
    shared = (
        lax.psum_scatter(grad_qkv, ("dp", "fsdp"), scatter_dimension=0, tiled=True),
        lax.psum_scatter(grad_out, ("dp", "fsdp"), scatter_dimension=0, tiled=True),
        lax.psum_scatter(grad_up, ("dp", "fsdp"), scatter_dimension=0, tiled=True),
        lax.psum_scatter(grad_down, ("dp", "fsdp"), scatter_dimension=0, tiled=True),
    )
    return (
        output,
        grad_tokens,
        grad_first,
        grad_vectors,
        shared[0],
        shared[1],
        shared[2],
        shared[3],
    )


def solution(mesh):
    placed = (
        P(("dp", "fsdp"), None),
        P(("dp", "fsdp"), None),
        P(("dp", "fsdp"), None),
        P(("dp", "fsdp"), None),
        P("fsdp"),
        P(("dp", "fsdp"), None),
        P(("dp", "fsdp"), None),
        P(("dp", "fsdp"), None),
        P(("dp", "fsdp"), None),
    )
    return jax.shard_map(
        local,
        mesh=mesh,
        in_specs=placed,
        out_specs=(
            P(("dp", "fsdp"), None),
            P(("dp", "fsdp"), None),
            P(("dp", "fsdp"), None),
            P("fsdp"),
            P(("dp", "fsdp"), None),
            P(("dp", "fsdp"), None),
            P(("dp", "fsdp"), None),
            P(("dp", "fsdp"), None),
        ),
        check_vma=False,
    )
```

profile of v0, /device:TPU:0, one launch (start us, length us, event | category | flops | bytes accessed | tf_op | source)
XLA Modules:
  0.0 898.6 jit_solution(15864918100808705275)
XLA Ops:
  12.8 26.2 %all-reduce = f32[8832]{0:T(1024)S(1)} all-reduce(f32[8832]{0:T(1024)S(1)} %dynamic-update-slice), channel_id=1, replica_groups=mesh['dp'=4,'fsdp'=8] {'fsdp'}, use_global_device_ids=true, to_apply=%add | all-reduce | flops 8832 | bytes 70656
  45.2 27.2 %all-gather.5.cloned.1.call-done = bf16[768,1920]{1,0:T(8,128)(2,1)} async-done(((bf16[24,1920]{1,0:T(8,128)(2,1)}), bf16[768,1920]{1,0:T(8,128)(2,1)}) %all-gather.5.cloned.1.call-update) | async-done | bytes 2949136 | tf_op jit(solution)/shard_map/all_gather | solution.py:149
  72.4 5.6 fusion.56
  78.2 2.9 copy-done.18
  83.0 3.3 fusion.44
  90.1 73.3 %while.29 = (s32[]{:T(128)}, bf16[2,512,12,64]{1,3,2,0:T(8,128)(2,1)}, f32[2,12,512,1]{2,1,3,0:T(8,128)S(1)}, s32[2]{0:T(128)S(1)}, s32[1024]{0:T(1024)S(1)}, /*...) while((s32[]{:T(128)}, ...), condition=%wide.region_5.6_spmd.clone, body=%wide.region_2.5_spmd.clone.sunk | while | flops 1687676928 | bytes 190296336 | solution.py:78
  92.1 10.7 %fusion.108 = (f32[12,512]{1,0:T(8,128)S(1)}, f32[12,512,1024]{2,1,0:T(8,128)}) fusion(pred[512,1024]{1,0:T(8,128)(4,1)S(1)} %compare_and_fusion.4, bf16[1024,12,64]{0,2,1:T(8,128)(2,1)S(1)} %get-tuple-element.507, bf16[1024,12,64]{0,2,1:T(8,128)(2,1)S(1)} %get-tuple-element.506, s32[]{:T(128)S(6)} %select_n.68), kind=kOutput, calls=%fused_computation.3.clone.1 | convolution fusion | flops 824174592 | bytes 28073988 | tf_op jit(solution)/shard_map/while/body/eval_jaxpr/qhd,khd->hqk/dot_general | solution.py:57
  102.8 12.3 %fusion.109 = f32[12,512]{1,0:T(8,128)S(1)} fusion(f32[12,512,1024]{2,1,0:T(8,128)} %get-tuple-element.458, f32[12,512]{1,0:T(8,128)S(1)} %get-tuple-element.459, pred[512,1024]{1,0:T(8,128)(4,1)S(1)} %compare_and_fusion.4), kind=kLoop, calls=%fused_computation.4.clone.1 | loop fusion | flops 25159680 | bytes 25739264 | tf_op jit(solution)/shard_map/while/body/eval_jaxpr/reduce_sum | solution.py:73
  115.1 3.2 copy-done
  118.3 8.5 bitcast_dynamic-update-slice_fusion.6
  128.7 10.8 %fusion.108 = (f32[12,512]{1,0:T(8,128)S(1)}, f32[12,512,1024]{2,1,0:T(8,128)}) fusion(pred[512,1024]{1,0:T(8,128)(4,1)S(1)} %compare_and_fusion.4, bf16[1024,12,64]{0,2,1:T(8,128)(2,1)S(1)} %get-tuple-element.507, bf16[1024,12,64]{0,2,1:T(8,128)(2,1)S(1)} %get-tuple-element.506, s32[]{:T(128)S(6)} %select_n.68), kind=kOutput, calls=%fused_computation.3.clone.1 | convolution fusion | flops 824174592 | bytes 28073988 | tf_op jit(solution)/shard_map/while/body/eval_jaxpr/qhd,khd->hqk/dot_general | solution.py:57
  139.5 12.3 %fusion.109 = f32[12,512]{1,0:T(8,128)S(1)} fusion(f32[12,512,1024]{2,1,0:T(8,128)} %get-tuple-element.458, f32[12,512]{1,0:T(8,128)S(1)} %get-tuple-element.459, pred[512,1024]{1,0:T(8,128)(4,1)S(1)} %compare_and_fusion.4), kind=kLoop, calls=%fused_computation.4.clone.1 | loop fusion | flops 25159680 | bytes 25739264 | tf_op jit(solution)/shard_map/while/body/eval_jaxpr/reduce_sum | solution.py:73
  151.8 3.1 copy-done
  154.9 8.5 bitcast_dynamic-update-slice_fusion.6
  163.5 3.0 copy.53
  168.1 3.9 fusion.65
  174.1 19.6 %all-gather.9.cloned.1.call-done = bf16[768,3072]{1,0:T(8,128)(2,1)} async-done(((bf16[24,3072]{1,0:T(8,128)(2,1)}), bf16[768,3072]{1,0:T(8,128)(2,1)}) %all-gather.9.cloned.1.call-update) | async-done | bytes 4718608 | tf_op jit(solution)/shard_map/all_gather | solution.py:151
  193.7 11.4 %fusion.59 = f32[1024,3072]{1,0:T(8,128)} fusion(bf16[768,3072]{1,0:T(8,128)(2,1)} %all-gather.9.cloned.1.call-done, f32[1024,768]{0,1:T(8,128)} %copy-done.6, f32[768]{0:T(1024)S(1)} %copy-done.33, f32[768]{0:T(1024)S(1)} %copy-done.29, f32[1024]{0:T(1024)S(1)} %fusion.52, f32[1024]{0:T(1024)S(1)} %broadcast_multiply_fusion), kind=kOutput, calls=%fused_computation.112 | convolution fusion | flops 4835770368 | bytes 20461568 | tf_op jit(solution)/shard_map/dot_general | solution.py:169
  205.1 53.8 %all-gather.11.cloned.1.call-done = bf16[3072,768]{1,0:T(8,128)(2,1)} async-done(((bf16[96,768]{1,0:T(8,128)(2,1)}), bf16[3072,768]{1,0:T(8,128)(2,1)}) %all-gather.11.cloned.1.call-update) | async-done | bytes 4718608 | tf_op jit(solution)/shard_map/all_gather | solution.py:152
  259.0 16.9 %convert_reduce_fusion = (f32[3072]{0:T(1024)}, bf16[1024,3072]{1,0:T(8,128)(2,1)S(1)}) fusion(f32[1024,3072]{1,0:T(8,128)} %fusion.59, f32[3072]{0:T(1024)S(1)} %copy-done.47, bf16[1024,768]{1,0:T(8,128)(2,1)} %param.15, bf16[3072,768]{1,0:T(8,128)(2,1)} %all-gather.11.cloned.1.call-done), kind=kOutput, calls=%fused_computation.46 | convolution fusion | flops 4904186880 | bytes 25190400 | tf_op jit(solution)/shard_map/dot_general | solution.py:34
  275.9 7.3 fusion.67
  283.2 3.5 copy.56
  286.7 4.5 multiply_reduce_fusion.1
  295.1 2.8 fusion.68
  298.0 4.4 convolution_convert_fusion
  303.7 175.8 %while.30 = (s32[]{:T(128)}, f32[1024,12,64]{0,2,1:T(8,128)}, f32[1024,12,64]{0,2,1:T(8,128)}, bf16[2,512,12,64]{1,3,2,0:T(8,128)(2,1)}, s32[2]{0:T(128)S(1)}, /...) while((s32[]{:T(128)}, f32[1024,12,64]{0,2,1:T(8,128)}, ...), condition=%wide.region_12.13_spmd.clone.clone, body=%wide.region_10.12_spmd.clone.clone.sunk | while | flops 4126795776 | bytes 231936368 | solution.py:120
  307.7 11.7 %fusion.119 = f32[12,512,1024]{2,1,0:T(8,128)} fusion(bf16[1024,12,64]{0,2,1:T(8,128)(2,1)S(1)} %get-tuple-element.555, bf16[1024,12,64]{0,2,1:T(8,128)(2,1)} %copy-done.1, s32[]{:T(128)S(6)} %select_n.72), kind=kOutput, calls=%fused_computation.28.clone.1 | convolution fusion | flops 805306368 | bytes 27525124 | tf_op jit(solution)/shard_map/while/body/eval_jaxpr/qhd,khd->hqk/dot_general | solution.py:57
  319.4 13.7 %bitcast_add_fusion.5 = f32[1024,12,64]{0,2,1:T(8,128)} fusion(f32[1024,12,64]{0,2,1:T(8,128)} %get-tuple-element.532, f32[12,512,1024]{2,1,0:T(8,128)} %fusion.119, f32[12,512]{1,0:T(8,128)S(1)} %dynamic-slice_bitcast_fusion.2, pred[512,1024]{1,0:T(8,128)(4,1)S(1)} %compare_and_fusion.5, pred[]{:T(512)S(6)} %compare.3, ...), kind=kOutput, calls=%fused_computation.20.clone.1 | convolution fusion | flops 832045056 | bytes 32800772 | tf_op jit(solution)/shard_map/while/body/eval_jaxpr/hqk,qhd->khd/dot_general | solution.py:95
  333.1 18.2 %multiply_reduce_fusion.5 = (f32[12,512]{1,0:T(8,128)S(1)}, f32[12,512,1024]{2,1,0:T(8,128)}) fusion(f32[12,512,1024]{2,1,0:T(8,128)} %fusion.119, f32[12,512]{1,0:T(8,128)S(1)} %dynamic-slice_bitcast_fusion.2, pred[512,1024]{1,0:T(8,128)(4,1)S(1)} %compare_and_fusion.5, bf16[1024,12,64]{0,2,1:T(8,128)(2,1)} %get-tuple-element.558, ...), kind=kOutput, calls=%fused_computation.15.clone.1 | convolution fusion | flops 836757504 | bytes 53264388 | tf_op jit(solution)/shard_map/while/body/eval_jaxpr/qhd,khd->hqk/dot_general | solution.py:101
  351.3 21.9 %multiply_convert_fusion.5 = bf16[12,512,1024]{2,1,0:T(8,128)(2,1)} fusion(f32[12,512,1024]{2,1,0:T(8,128)} %get-tuple-element.472, f32[12,512,1024]{2,1,0:T(8,128)} %fusion.119, f32[12,512]{1,0:T(8,128)S(1)} %get-tuple-element.473, f32[12,512]{1,0:T(8,128)S(1)} %dynamic-slice_bitcast_fusion.2, pred[512,1024]{1,0:T(8,128)(4,1)S(1)} %compare_and_fusion.5), kind=kLoop, calls=%fused_computation.14.clone.1 | loop fusion | flops 37748736 | bytes 63488000 | tf_op jit(solution)/shard_map/while/body/eval_jaxpr/convert_element_type | solution.py:105
  373.3 9.6 %bitcast_dynamic-update-slice_fusion.8 = bf16[2,512,12,64]{1,3,2,0:T(8,128)(2,1)} fusion(bf16[2,512,12,64]{1,3,2,0:T(8,128)(2,1)} %get-tuple-element.533, s32[]{:T(128)S(6)} %copy.84, bf16[12,512,1024]{2,1,0:T(8,128)(2,1)} %multiply_convert_fusion.5, bf16[1024,12,64]{0,2,1:T(8,128)(2,1)S(1)} %get-tuple-element.555), kind=kOutput, calls=%fused_computation.23.clone.1 | convolution fusion | flops 805699584 | bytes 15728644 | tf_op jit(solution)/shard_map/while/body/eval_jaxpr/hqk,khd->qhd/dot_general | solution.py:107
  382.9 8.5 bitcast_add_fusion.4
  395.2 11.5 %fusion.119 = f32[12,512,1024]{2,1,0:T(8,128)} fusion(bf16[1024,12,64]{0,2,1:T(8,128)(2,1)S(1)} %get-tuple-element.555, bf16[1024,12,64]{0,2,1:T(8,128)(2,1)} %copy-done.1, s32[]{:T(128)S(6)} %select_n.72), kind=kOutput, calls=%fused_computation.28.clone.1 | convolution fusion | flops 805306368 | bytes 27525124 | tf_op jit(solution)/shard_map/while/body/eval_jaxpr/qhd,khd->hqk/dot_general | solution.py:57
  406.6 14.3 %bitcast_add_fusion.5 = f32[1024,12,64]{0,2,1:T(8,128)} fusion(f32[1024,12,64]{0,2,1:T(8,128)} %get-tuple-element.532, f32[12,512,1024]{2,1,0:T(8,128)} %fusion.119, f32[12,512]{1,0:T(8,128)S(1)} %dynamic-slice_bitcast_fusion.2, pred[512,1024]{1,0:T(8,128)(4,1)S(1)} %compare_and_fusion.5, pred[]{:T(512)S(6)} %compare.3, ...), kind=kOutput, calls=%fused_computation.20.clone.1 | convolution fusion | flops 832045056 | bytes 32800772 | tf_op jit(solution)/shard_map/while/body/eval_jaxpr/hqk,qhd->khd/dot_general | solution.py:95
  421.0 18.1 %multiply_reduce_fusion.5 = (f32[12,512]{1,0:T(8,128)S(1)}, f32[12,512,1024]{2,1,0:T(8,128)}) fusion(f32[12,512,1024]{2,1,0:T(8,128)} %fusion.119, f32[12,512]{1,0:T(8,128)S(1)} %dynamic-slice_bitcast_fusion.2, pred[512,1024]{1,0:T(8,128)(4,1)S(1)} %compare_and_fusion.5, bf16[1024,12,64]{0,2,1:T(8,128)(2,1)} %get-tuple-element.558, ...), kind=kOutput, calls=%fused_computation.15.clone.1 | convolution fusion | flops 836757504 | bytes 53264388 | tf_op jit(solution)/shard_map/while/body/eval_jaxpr/qhd,khd->hqk/dot_general | solution.py:101
  439.1 21.2 %multiply_convert_fusion.5 = bf16[12,512,1024]{2,1,0:T(8,128)(2,1)} fusion(f32[12,512,1024]{2,1,0:T(8,128)} %get-tuple-element.472, f32[12,512,1024]{2,1,0:T(8,128)} %fusion.119, f32[12,512]{1,0:T(8,128)S(1)} %get-tuple-element.473, f32[12,512]{1,0:T(8,128)S(1)} %dynamic-slice_bitcast_fusion.2, pred[512,1024]{1,0:T(8,128)(4,1)S(1)} %compare_and_fusion.5), kind=kLoop, calls=%fused_computation.14.clone.1 | loop fusion | flops 37748736 | bytes 63488000 | tf_op jit(solution)/shard_map/while/body/eval_jaxpr/convert_element_type | solution.py:105
  460.3 9.5 %bitcast_dynamic-update-slice_fusion.8 = bf16[2,512,12,64]{1,3,2,0:T(8,128)(2,1)} fusion(bf16[2,512,12,64]{1,3,2,0:T(8,128)(2,1)} %get-tuple-element.533, s32[]{:T(128)S(6)} %copy.84, bf16[12,512,1024]{2,1,0:T(8,128)(2,1)} %multiply_convert_fusion.5, bf16[1024,12,64]{0,2,1:T(8,128)(2,1)S(1)} %get-tuple-element.555), kind=kOutput, calls=%fused_computation.23.clone.1 | convolution fusion | flops 805699584 | bytes 15728644 | tf_op jit(solution)/shard_map/while/body/eval_jaxpr/hqk,khd->qhd/dot_general | solution.py:107
  469.8 9.4 %bitcast_add_fusion.4 = f32[1024,12,64]{0,2,1:T(8,128)} fusion(f32[1024,12,64]{0,2,1:T(8,128)} %get-tuple-element.531, bf16[12,512,1024]{2,1,0:T(8,128)(2,1)} %multiply_convert_fusion.5, pred[]{:T(512)S(6)} %compare.3, bf16[1024,12,64]{0,2,1:T(8,128)(2,1)S(1)} %copy-done.2, s32[]{:T(128)S(6)} %select_n.72), kind=kOutput, calls=%fused_computation.21.clone.1 | convolution fusion | flops 807665664 | bytes 19660804 | tf_op jit(solution)/shard_map/while/body/eval_jaxpr/hqk,qhd->khd/dot_general | solution.py:112
  489.7 6.1 fusion.46
  496.5 13.3 %fusion.60 = f32[3072,768]{1,0:T(8,128)} fusion(bf16[1024,768]{1,0:T(8,128)(2,1)} %param.15, f32[1024,3072]{1,0:T(8,128)} %fusion.59, f32[3072]{0:T(1024)S(1)} %copy-done.48), kind=kOutput, calls=%fused_computation.113 | convolution fusion | flops 4863295488 | bytes 23605248 | tf_op jit(solution)/shard_map/dot_general | solution.py:28
  510.6 11.2 %fusion.58 = f32[768,3072]{1,0:T(8,128)} fusion(bf16[1024,3072]{1,0:T(8,128)(2,1)} %copy-done.55, f32[1024,768]{0,1:T(8,128)} %copy-done.6, f32[768]{0:T(1024)S(1)} %copy-done.34, f32[768]{0:T(1024)S(1)} %copy-done.30, f32[1024]{0:T(1024)S(1)} %copy-done.32, f32[1024]{0:T(1024)S(1)} %copy-done.28), kind=kOutput, calls=%fused_computation.111 | convolution fusion | flops 4835770368 | bytes 18888704 | tf_op jit(solution)/shard_map/dot_general | solution.py:28
  522.4 12.6 %add_convert_fusion.1 = bf16[1024,768]{0,1:T(8,128)(2,1)} fusion(f32[1024,768]{0,1:T(8,128)} %copy-done.6, bf16[3072,768]{1,0:T(8,128)(2,1)} %all-gather.11.cloned.1.call-done, f32[768]{0:T(1024)S(1)} %copy-done.50, f32[1024,3072]{1,0:T(8,128)} %fusion.59, f32[3072]{0:T(1024)S(1)} %copy-done.48), kind=kOutput, calls=%fused_computation.75 | convolution fusion | flops 4865654784 | bytes 22035456 | tf_op jit(solution)/shard_map/dot_general | solution.py:173
  540.2 8.2 fusion.66
  548.4 3.7 copy.58
  560.7 40.8 %psum.7 = f32[8832]{0:T(1024)S(1)} all-reduce(f32[8832]{0:T(1024)S(1)} %constant_dynamic-update-slice_fusion), channel_id=1, replica_groups=mesh['dp'=4,'fsdp'=8] {'dp','fsdp'}, use_global_device_ids=true, to_apply=%region_24.25 | all-reduce | flops 8832 | bytes 70656 | tf_op jit(solution)/shard_map/psum | solution.py:222
  602.2 5.9 reduce-scatter.13.cloned.1.call-done
  608.1 142.4 %reduce-scatter.11.cloned.1.call-done = f32[96,768]{1,0:T(8,128)} async-done(((f32[3072,768]{1,0:T(8,128)}), f32[96,768]{1,0:T(8,128)}) %reduce-scatter.11.cloned.1.call-update) | async-done | bytes 294928 | tf_op jit(solution)/shard_map/reduce_scatter | solution.py:229
  750.5 141.1 %reduce-scatter.9.cloned.1.call-done = f32[24,3072]{1,0:T(8,128)} async-done(((f32[768,3072]{1,0:T(8,128)}), f32[24,3072]{1,0:T(8,128)}) %reduce-scatter.9.cloned.1.call-update) | async-done | bytes 294928 | tf_op jit(solution)/shard_map/reduce_scatter | solution.py:228
  (220 shorter events, 57.6 us)
Async XLA Ops:
  7.2 65.2 %all-gather.5.cloned.1.call-start = ((), (), s32[]{:S(2)}) async-start(), calls=%async_computation.4 | async-start | bytes 3041280 | tf_op jit(solution)/shard_map/all_gather | solution.py:149
  7.9 160.2 %all-gather.7.cloned.1.call-start = ((), (), s32[]{:S(2)}) async-start(), calls=%async_computation.5 | async-start | bytes 1216512 | tf_op jit(solution)/shard_map/all_gather | solution.py:150
  8.6 185.1 %all-gather.9.cloned.1.call-start = ((), (), s32[]{:S(2)}) async-start(), calls=%async_computation.6 | async-start | bytes 4866048 | tf_op jit(solution)/shard_map/all_gather | solution.py:151
  9.4 249.6 %all-gather.11.cloned.1.call-start = ((), (), s32[]{:S(2)}) async-start(), calls=%async_computation.7 | async-start | bytes 4866048 | tf_op jit(solution)/shard_map/all_gather | solution.py:152
  10.0 592.2 %reduce-scatter.7.cloned.1.call-start = ((), (), s32[]{:S(2)}) async-start(), calls=%async_computation.8 | async-start | bytes 2433024 | tf_op jit(solution)/shard_map/reduce_scatter | solution.py:227
  40.2 32.2 %copy-start.37 = (f32[768]{0:T(1024)}, f32[768]{0:T(1024)S(1)}, u32[]{:S(2)}) copy-start(f32[768]{0:T(1024)S(1)} %get-tuple-element.328) | copy-start | bytes 9220
  40.2 32.2 %copy-start.51 = (f32[768]{0:T(1024)}, f32[768]{0:T(1024)S(1)}, u32[]{:S(2)}) copy-start(f32[768]{0:T(1024)S(1)} %get-tuple-element.327) | copy-start | bytes 9220
  40.9 2.6 copy-start.20
  42.8 29.7 %copy-start.4 = (bf16[1024,768]{0,1:T(8,128)(2,1)}, bf16[1024,768]{0,1:T(8,128)(2,1)S(1)}, u32[]{:S(2)}) copy-start(bf16[1024,768]{0,1:T(8,128)(2,1)S(1)} %copy.49) | copy-start | bytes 4718596
  43.0 35.0 %copy-start.35 = (f32[1024]{0:T(1024)}, f32[1024]{0:T(1024)S(1)}, u32[]{:S(2)}) copy-start(f32[1024]{0:T(1024)S(1)} %broadcast_multiply_fusion.1) | copy-start | bytes 12292
  43.5 34.5 %copy-start.43 = (f32[1024]{0:T(1024)}, f32[1024]{0:T(1024)S(1)}, u32[]{:S(2)}) copy-start(f32[1024]{0:T(1024)S(1)} %fusion.42) | copy-start | bytes 12292
  43.5 34.5 %copy-start.39 = (f32[1024]{0:T(1024)}, f32[1024]{0:T(1024)S(1)}, u32[]{:S(2)}) copy-start(f32[1024]{0:T(1024)S(1)} %fusion.51) | copy-start | bytes 12292
  78.1 3.0 copy-start.18
  78.1 3.2 copy-start.25
  92.1 23.0 %copy-start.3 = (bf16[1024,12,64]{0,2,1:T(8,128)(2,1)S(1)}, bf16[1024,12,64]{0,2,1:T(8,128)(2,1)}, u32[]{:S(2)}) copy-start(bf16[1024,12,64]{0,2,1:T(8,128)(2,1)} %get-tuple-element.508) | copy-start | bytes 4718596 | tf_op jit(solution)/shard_map/while
  102.8 15.6 %copy-start = (f32[12,512,1024]{2,1,0:T(8,128)S(1)}, f32[12,512,1024]{2,1,0:T(8,128)}, u32[]{:S(2)}) copy-start(f32[12,512,1024]{2,1,0:T(8,128)} %get-tuple-element.458) | copy-start | bytes 75497472 | tf_op jit(solution)/shard_map/while
  128.7 23.2 %copy-start.3 = (bf16[1024,12,64]{0,2,1:T(8,128)(2,1)S(1)}, bf16[1024,12,64]{0,2,1:T(8,128)(2,1)}, u32[]{:S(2)}) copy-start(bf16[1024,12,64]{0,2,1:T(8,128)(2,1)} %get-tuple-element.508) | copy-start | bytes 4718596 | tf_op jit(solution)/shard_map/while
  139.5 15.4 %copy-start = (f32[12,512,1024]{2,1,0:T(8,128)S(1)}, f32[12,512,1024]{2,1,0:T(8,128)}, u32[]{:S(2)}) copy-start(f32[12,512,1024]{2,1,0:T(8,128)} %get-tuple-element.458) | copy-start | bytes 75497472 | tf_op jit(solution)/shard_map/while
  163.4 4.6 copy-start.53
  172.0 21.7 %copy-start.29 = (f32[768]{0:T(1024)S(1)}, f32[768]{0:T(1024)}, u32[]{:S(2)}) copy-start(f32[768]{0:T(1024)} %get-tuple-element.323) | copy-start | bytes 9220
  172.0 21.7 %copy-start.33 = (f32[768]{0:T(1024)S(1)}, f32[768]{0:T(1024)}, u32[]{:S(2)}) copy-start(f32[768]{0:T(1024)} %get-tuple-element.324) | copy-start | bytes 9220
  172.0 119.2 %copy-start.27 = (f32[1024]{0:T(1024)}, f32[1024]{0:T(1024)S(1)}, u32[]{:S(2)}) copy-start(f32[1024]{0:T(1024)S(1)} %broadcast_multiply_fusion) | copy-start | bytes 12292
  174.1 117.1 %copy-start.31 = (f32[1024]{0:T(1024)}, f32[1024]{0:T(1024)S(1)}, u32[]{:S(2)}) copy-start(f32[1024]{0:T(1024)S(1)} %fusion.52) | copy-start | bytes 12292
  193.7 65.2 %copy-start.47 = (f32[3072]{0:T(1024)S(1)}, f32[3072]{0:T(1024)}, u32[]{:S(2)}) copy-start(f32[3072]{0:T(1024)} %slice.73) | copy-start | bytes 36868
  259.0 17.0 %copy-start.19 = (bf16[768,3072]{1,0:T(8,128)(2,1)S(1)}, bf16[768,3072]{1,0:T(8,128)(2,1)}, u32[]{:S(2)}) copy-start(bf16[768,3072]{1,0:T(8,128)(2,1)} %all-gather.9.cloned.1.call-done) | copy-start | bytes 14155780
  275.9 7.3 copy-start.55
  286.7 4.5 copy-start.7
  286.7 4.7 copy-start.11
  298.0 310.1 %reduce-scatter.13.cloned.1.call-start = ((), (), s32[]{:S(2)}) async-start(), calls=%async_computation.11 | async-start | bytes 6082560
  303.9 3.3 copy-start.1
  307.7 11.7 %copy-start.17 = (bf16[1024,12,64]{0,2,1:T(8,128)(2,1)S(1)}, bf16[1024,12,64]{0,2,1:T(8,128)(2,1)}, u32[]{:S(2)}) copy-start(bf16[1024,12,64]{0,2,1:T(8,128)(2,1)} %get-tuple-element.557) | copy-start | bytes 4718596 | tf_op jit(solution)/shard_map/while
  373.3 9.6 %copy-start.2 = (bf16[1024,12,64]{0,2,1:T(8,128)(2,1)S(1)}, bf16[1024,12,64]{0,2,1:T(8,128)(2,1)}, u32[]{:S(2)}) copy-start(bf16[1024,12,64]{0,2,1:T(8,128)(2,1)} %copy-done.1) | copy-start | bytes 4718596 | tf_op jit(solution)/shard_map/while
  391.4 3.3 copy-start.1
  395.2 11.5 %copy-start.17 = (bf16[1024,12,64]{0,2,1:T(8,128)(2,1)S(1)}, bf16[1024,12,64]{0,2,1:T(8,128)(2,1)}, u32[]{:S(2)}) copy-start(bf16[1024,12,64]{0,2,1:T(8,128)(2,1)} %get-tuple-element.557) | copy-start | bytes 4718596 | tf_op jit(solution)/shard_map/while
  460.3 9.5 %copy-start.2 = (bf16[1024,12,64]{0,2,1:T(8,128)(2,1)S(1)}, bf16[1024,12,64]{0,2,1:T(8,128)(2,1)}, u32[]{:S(2)}) copy-start(bf16[1024,12,64]{0,2,1:T(8,128)(2,1)} %copy-done.1) | copy-start | bytes 4718596 | tf_op jit(solution)/shard_map/while
  479.5 2.4 copy-start.12
  481.7 7.1 copy-start.23
  483.9 4.9 copy-start.21
  483.9 5.8 copy-start.5
  483.9 5.8 copy-start.36
  483.9 5.8 copy-start.38
  483.9 5.8 copy-start.40
  483.9 5.8 copy-start.52
  495.9 254.6 %reduce-scatter.11.cloned.1.call-start = ((), (), s32[]{:S(2)}) async-start(), calls=%async_computation.10 | async-start | bytes 9732096 | tf_op jit(solution)/shard_map/reduce_scatter | solution.py:229
  509.9 381.7 %reduce-scatter.9.cloned.1.call-start = ((), (), s32[]{:S(2)}) async-start(), calls=%async_computation.9 | async-start | bytes 9732096 | tf_op jit(solution)/shard_map/reduce_scatter | solution.py:228
  552.1 2.6 copy-start.44
  552.1 2.8 copy-start.8
  554.7 2.4 copy-start.14
  (21 other events, 29.7 us)
Sparse Core Ops, SparseCore 0:
  10.9 61.4 all-gather.4
  75.3 53.0 all-gather.6
  131.3 62.3 all-gather.8
  196.5 62.4 all-gather.10
  298.1 97.8 reduce-scatter.6
  496.0 112.0 reduce-scatter.12
  615.6 134.8 reduce-scatter.10
  756.9 134.6 reduce-scatter.8
where the time goes:
time: 905 us; the launch traced here: 899 us
  waiting for transfers between devices  393 us (43%)
  matrix products  267 us (30%)
  other arithmetic  92.6 us (10%)
  blocking collectives  66.9 us (7%)
  local copies, waits for them, and re-layouts  57 us (6%)
  between operations  15.7 us (2%)
    reduce_scatter x1, waiting for transfers between devices, local(): lax.psum_scatter(grad_down, ('dp', 'fsdp'), scatter_dimension=0, tiled=True)  142 us
    reduce_scatter x1, waiting for transfers between devices, local(): lax.psum_scatter(grad_up, ('dp', 'fsdp'), scatter_dimension=0, tiled=True)  141 us
    all_gather x1, waiting for transfers between devices, local(): lax.all_gather(w_down, ('dp', 'fsdp'), axis=0, tiled=True)  53.8 us
    dot_general x4, matrix products, block_scores(): jnp.einsum('qhd,khd->hqk', part_query, keys, preferred_element_type=jnp.f...  44.7 us
    convert_element_type x2, other arithmetic, one_block(): grad_scores = (probs * (grad_probs - inner)).astype(jnp.bfloat16)  43.2 us
    psum x1, blocking collectives, local(): summed_vector = lax.psum(grad_vector, ('dp', 'fsdp'))  40.8 us
    dot_general x4, matrix products, right_dot(): lax.dot_general(left, right, (((1,), (1,)), ((), ())), preferred_element_...  36.8 us
    dot_general x2, matrix products, one_block(): jnp.einsum('qhd,khd->hqk', part_grad, values, preferred_element_type=jnp....  36.3 us
  transfers between devices with their start and end apart: 8, of which 6 were waited for; matrix products, arithmetic and copies ran while one was open for 40% of the time, Pallas kernels for 0%

commit v1 on v0

v1 whole, which is shorter than its diff:
```python
import functools, math
import jax
import jax.numpy as jnp
from jax.sharding import PartitionSpec as P
from jax import lax
from jax.experimental import pallas as pl
from jax.experimental.pallas import tpu as pltpu
BF=jnp.bfloat16; F32=jnp.float32
HD=64
NEG=-1e30
def nt(a,b): return lax.dot_general(a,b,(((1,),(1,)),((),())),preferred_element_type=F32)
def nn(a,b): return jnp.dot(a,b,preferred_element_type=F32)

def half_mask(head, n=128):
    return (lax.broadcasted_iota(jnp.int32,(1,n),1)//HD)==head

def attend_forward_kernel(len_ref, q_ref, k_ref, v_ref, o_ref, lse_ref, ot_ref):
    rows=q_ref.shape[0]; blk=256; half=rows//2
    bias=jnp.where(len_ref[0,0]<rows, NEG, 0.0).astype(F32)
    vt=v_ref[...].T
    causal=lax.broadcasted_iota(jnp.int32,(blk,blk),0)<=lax.broadcasted_iota(jnp.int32,(blk,blk),1)
    for head in range(2):
        vth=vt[HD*head:HD*head+HD]
        for i in range(rows//blk):
            q=jnp.where(half_mask(head), q_ref[i*blk:(i+1)*blk], jnp.zeros((),BF))
            parts=[]
            for j in range(i+1):
                s=nt(k_ref[j*blk:(j+1)*blk], q)
                if j==i: s=jnp.where(causal,s,NEG)
                elif i*blk>=half and (j+1)*blk<=half: s=s+bias
                parts.append(s)
            m=parts[0].max(axis=0,keepdims=True)
            for s in parts[1:]: m=jnp.maximum(m,s.max(axis=0,keepdims=True))
            l=jnp.zeros((1,blk),F32); ot=jnp.zeros((HD,blk),F32)
            for j,s in enumerate(parts):
                p=jnp.exp(s-m)
                l=l+p.sum(axis=0,keepdims=True)
                ot=ot+nn(vth[:,j*blk:(j+1)*blk],p.astype(BF))
            ot_ref[HD*head:HD*head+HD,i*blk:(i+1)*blk]=ot/l
            lse_ref[0,head:head+1,i*blk:(i+1)*blk]=m+jnp.log(l)
    o_ref[...]=ot_ref[...].T.astype(BF)

def attend_forward(lengths,q,k,v):
    rows,width=q.shape
    pair=pl.BlockSpec((rows,128),lambda p:(0,p))
    n=width//128
    return pl.pallas_call(attend_forward_kernel,grid=(n,),
        in_specs=[pl.BlockSpec(memory_space=pltpu.SMEM),pair,pair,pair],
        out_specs=[pair,pl.BlockSpec((1,2,rows),lambda p:(p,0,0))],
        out_shape=[jax.ShapeDtypeStruct((rows,width),BF),jax.ShapeDtypeStruct((n,2,rows),F32)],
        scratch_shapes=[pltpu.VMEM((128,rows),F32)],
        compiler_params=pltpu.CompilerParams(vmem_limit_bytes=48<<20),
        cost_estimate=pl.CostEstimate(flops=4*rows*rows*width,bytes_accessed=8*rows*width,transcendentals=rows*rows*width//64),
        name="attend_forward")(lengths,q,k,v)

def attend_backward_kernel(len_ref,q_ref,k_ref,v_ref,o_ref,do_ref,lse_ref,dq_ref,dk_ref,df_ref,gf_ref,dqt_ref,dv_ref,dk_acc,nfresh=3):
    rows=q_ref.shape[0]; blk=256; half=rows//2
    pair=pl.program_id(0)
    bias=jnp.where(len_ref[0,0]<rows, NEG, 0.0).astype(F32)
    prod=(do_ref[...].astype(F32)*o_ref[...].astype(F32)).T
    kt=k_ref[...].T
    causal=lax.broadcasted_iota(jnp.int32,(blk,blk),0)<=lax.broadcasted_iota(jnp.int32,(blk,blk),1)
    nb=rows//blk
    for head in range(2):
        delta=prod[HD*head:HD*head+HD].sum(axis=0,keepdims=True)
        lse=lse_ref[0,head:head+1,:]
        qh=jnp.where(half_mask(head), q_ref[...], jnp.zeros((),BF))
        doh=jnp.where(half_mask(head), do_ref[...], jnp.zeros((),BF))
        for j in range(nb):
            kj=k_ref[j*blk:(j+1)*blk]; vj=v_ref[j*blk:(j+1)*blk]
            ktj=kt[HD*head:HD*head+HD,j*blk:(j+1)*blk]
            dv=jnp.zeros((blk,128),F32); dk=jnp.zeros((blk,128),F32)
            for i in range(j,nb):
                sl=slice(i*blk,(i+1)*blk)
                s=nt(kj,qh[sl])
                if i==j: s=jnp.where(causal,s,NEG)
                elif i*blk>=half and (j+1)*blk<=half: s=s+bias
                p=jnp.exp(s-lse[:,sl])
                dp=nt(vj,doh[sl])
                ds=(p*(dp-delta[:,sl])).astype(BF)
                dv=dv+nn(p.astype(BF),doh[sl])
                dk=dk+nn(ds,qh[sl])
                dqt=nn(ktj,ds)
                if j==0: dqt_ref[HD*head:HD*head+HD,sl]=dqt
                else: dqt_ref[HD*head:HD*head+HD,sl]+=dqt
            kr=slice(j*blk,(j+1)*blk)
            if head==0:
                dv_ref[kr]=dv; dk_acc[kr]=dk
            else:
                dv_ref[kr]+=dv; dk_acc[kr]+=dk
    dq_ref[...]=(dqt_ref[...].T*0.125).astype(BF)
    dk_ref[...]=dk_acc[...].astype(BF)
    dv=dv_ref[...].astype(BF)
    @pl.when(pair<nfresh)
    def _(): df_ref[...]=dv
    @pl.when(pair>=nfresh)
    def _(): gf_ref[...]=dv

def attend_backward(lengths,q,k,v,o,do,lse):
    rows,width=q.shape
    pair=pl.BlockSpec((rows,128),lambda p:(0,p))
    n=width//128; nf=n//2
    return pl.pallas_call(functools.partial(attend_backward_kernel,nfresh=nf),grid=(n,),
        in_specs=[pl.BlockSpec(memory_space=pltpu.SMEM)]+[pair]*5+[pl.BlockSpec((1,2,rows),lambda p:(p,0,0))],
        out_specs=[pair,pair,pl.BlockSpec((rows,128),lambda p:(0,jnp.minimum(p,nf-1))),pl.BlockSpec((rows,128),lambda p:(0,jnp.maximum(p-nf,0)))],
        out_shape=[jax.ShapeDtypeStruct((rows,width),BF)]*2+[jax.ShapeDtypeStruct((rows,width//2),BF)]*2,
        scratch_shapes=[pltpu.VMEM((128,rows),F32),pltpu.VMEM((rows,128),F32),pltpu.VMEM((rows,128),F32)],
        compiler_params=pltpu.CompilerParams(vmem_limit_bytes=48<<20),
        cost_estimate=pl.CostEstimate(flops=10*rows*rows*width,bytes_accessed=16*rows*width,transcendentals=rows*rows*width//64),
        name="attend_backward")(lengths,q,k,v,o,do,lse)

def row_stats(v):
    center=v-jnp.mean(v,axis=-1,keepdims=True)
    rstd=lax.rsqrt(jnp.mean(center*center,axis=-1,keepdims=True)+1e-5)
    return center*rstd, rstd

def project_kernel(x_ref,first_ref,g_ref,b_ref,bq_ref,bv_ref,w_ref,a_ref,q_ref,k_ref,v_ref):
    d=x_ref.shape[1]; vd=first_ref.shape[1]
    xh,_=row_stats(x_ref[...].astype(F32))
    a=(xh*g_ref[...]+b_ref[...]).astype(BF)
    a_ref[...]=a
    q=(nn(a,w_ref[:,0:d])+bq_ref[...]).astype(BF)
    q_ref[...]=(q.astype(F32)*0.125).astype(BF)
    k_ref[...]=nn(a,w_ref[:,d:2*d]).astype(BF)
    v_ref[:,0:vd]=(nn(a,w_ref[:,2*d:])+bv_ref[...]).astype(BF)
    v_ref[:,vd:]=first_ref[...]

def full(a):
    return pl.BlockSpec(a.shape,lambda i:(0,)*a.ndim,pipeline_mode=pl.Buffered(1))

def project(x,first,g,b,bq,bv,w,blk=256):
    rows,d=x.shape
    rb=lambda n: pl.BlockSpec((blk,n),lambda i:(i,0))
    return pl.pallas_call(project_kernel,grid=(rows//blk,),
        in_specs=[rb(d),rb(first.shape[1]),full(g),full(b),full(bq),full(bv),full(w)],
        out_specs=[rb(d)]*4,out_shape=[jax.ShapeDtypeStruct((rows,d),BF)]*4,
        compiler_params=pltpu.CompilerParams(vmem_limit_bytes=48<<20),
        cost_estimate=pl.CostEstimate(flops=2*rows*w.shape[0]*w.shape[1],bytes_accessed=2*rows*d*5+w.size*2,transcendentals=0),
        name="project")(x,first,g,b,bq,bv,w)

C0=math.sqrt(2/math.pi)
def mlp_kernel(o_ref,x_ref,c_ref,bo_ref,g_ref,b_ref,bu_ref,bd_ref,wo_ref,wu_ref,wd_ref,
               out_ref,a_ref,y_ref,du_ref,dx_ref,dz_ref,do_ref,dbo_ref,dg_ref,db_ref,dbu_ref,dbd_ref,chunk=512):
    step=pl.program_id(0)
    @pl.when(step==0)
    def _():
        for r in (dbo_ref,dg_ref,db_ref,dbu_ref,dbd_ref): r[...]=jnp.zeros(r.shape,F32)
    ff=wu_ref.shape[1]
    x1=x_ref[...].astype(F32)+(nn(o_ref[...],wo_ref[...])+bo_ref[...])
    xh,rstd=row_stats(x1)
    a=(xh*g_ref[...]+b_ref[...]).astype(BF)
    a_ref[...]=a
    c=c_ref[...]
    acc=x1+bd_ref[...]
    da=jnp.zeros(acc.shape,F32)
    for s in range(0,ff,chunk):
        sl=slice(s,s+chunk)
        u=nn(a,wu_ref[:,sl])+bu_ref[:,sl]
        dy=nt(c,wd_ref[sl])
        u2=u*u
        t=jnp.tanh(u*(C0+(C0*0.044715)*u2))
        h=0.5*t+0.5
        y=(u*h).astype(BF)
        y_ref[:,sl]=y
        acc=acc+nn(y,wd_ref[sl])
        gd=h+(0.5*u)*(1.0-t*t)*(C0+(3*C0*0.044715)*u2)
        du=(gd*dy).astype(BF)
        du_ref[:,sl]=du
        dbu_ref[:,sl]+=du.astype(F32).sum(axis=0,keepdims=True)
        da=da+nt(du,wu_ref[:,sl])
    out_ref[...]=acc.astype(BF)
    c32=c.astype(F32)
    dbd_ref[...]+=c32.sum(axis=0,keepdims=True)
    db_ref[...]+=da.sum(axis=0,keepdims=True)
    dg_ref[...]+=(da*xh).sum(axis=0,keepdims=True)
    dxh=da*g_ref[...]
    dx=c32+rstd*(dxh-jnp.mean(dxh,axis=-1,keepdims=True)-xh*jnp.mean(dxh*xh,axis=-1,keepdims=True))
    dx_ref[...]=dx
    dz=dx.astype(BF)
    dz_ref[...]=dz
    dbo_ref[...]+=dz.astype(F32).sum(axis=0,keepdims=True)
    do_ref[...]=nt(dz,wo_ref[...]).astype(BF)

def mlp(o,x,c,bo,g,b,bu,bd,wo,wu,wd,blk=256):
    rows,d=x.shape; ff=wu.shape[1]
    rb=lambda n: pl.BlockSpec((blk,n),lambda i:(i,0))
    vec=lambda n: pl.BlockSpec((1,n),lambda i:(0,0))
    S=jax.ShapeDtypeStruct
    return pl.pallas_call(mlp_kernel,grid=(rows//blk,),
        in_specs=[rb(d)]*3+[full(t) for t in (bo,g,b,bu,bd,wo,wu,wd)],
        out_specs=[rb(d),rb(d),rb(ff),rb(ff),rb(d),rb(d),rb(d),vec(d),vec(d),vec(d),vec(ff),vec(d)],
        out_shape=[S((rows,d),BF),S((rows,d),BF),S((rows,ff),BF),S((rows,ff),BF),S((rows,d),F32),S((rows,d),BF),S((rows,d),BF),
                   S((1,d),F32),S((1,d),F32),S((1,d),F32),S((1,ff),F32),S((1,d),F32)],
        compiler_params=pltpu.CompilerParams(vmem_limit_bytes=56<<20),
        cost_estimate=pl.CostEstimate(flops=4*rows*(wo.size+2*wu.size),bytes_accessed=rows*(d*18+ff*4)+2*(wo.size+2*wu.size),transcendentals=rows*ff),
        name="feed_forward")(o,x,c,bo,g,b,bu,bd,wo,wu,wd)

def grad_kernel(where_ref,l_ref,r_ref,own_ref,sib_ref,lt_ref,*,planes,zs,piece):
    z=where_ref[0]; pn=where_ref[1]; core=where_ref[2]
    @pl.when(pl.program_id(0)==0)
    def _(): lt_ref[...]=l_ref[...].T
    acc=nn(lt_ref[...],r_ref[...])
    for dz in range(zs):
        for dp in range(planes):
            base=(dz*planes+dp)*2*piece
            sz=lax.rem(dz-z+zs,zs); sp=jnp.bitwise_xor(dp,pn)
            lo=acc[base:base+piece].astype(BF); hi=acc[base+piece:base+2*piece].astype(BF)
            own_ref[sp,sz]=jnp.where(core==0,lo,hi)
            sib_ref[sp,sz]=jnp.where(core==0,hi,lo)

def weight_grad(where,left,right,planes,zs,nblk,name):
    rows,m=left.shape; n=right.shape[1]
    piece=m//(planes*zs*2)
    S=jax.ShapeDtypeStruct
    ob=pl.BlockSpec((planes,zs,piece,nblk),lambda i:(0,0,0,i))
    return pl.pallas_call(functools.partial(grad_kernel,planes=planes,zs=zs,piece=piece),grid=(n//nblk,),
        in_specs=[pl.BlockSpec(memory_space=pltpu.SMEM),full(left),pl.BlockSpec((rows,nblk),lambda i:(0,i))],
        out_specs=[ob,ob],out_shape=[S((planes,zs,piece,n),BF)]*2,
        scratch_shapes=[pltpu.VMEM((m,rows),BF)],
        compiler_params=pltpu.CompilerParams(vmem_limit_bytes=56<<20),
        cost_estimate=pl.CostEstimate(flops=2*rows*m*n,bytes_accessed=2*(left.size+right.size+m*n),transcendentals=0),
        name=name)(where,left,right)

def last_kernel(dq_ref,dk_ref,df_ref,w_ref,x_ref,dx_ref,g_ref,gt_ref,dg_ref,db_ref,dbq_ref,dbv_ref):
    d=x_ref.shape[1]
    @pl.when(pl.program_id(0)==0)
    def _():
        for r in (dg_ref,db_ref,dbq_ref,dbv_ref): r[...]=jnp.zeros(r.shape,F32)
    dq=dq_ref[...]; df=df_ref[...]
    da=nt(dq,w_ref[:,0:d])+nt(dk_ref[...],w_ref[:,d:2*d])+nt(df,w_ref[:,2*d:])
    dbq_ref[...]+=dq.astype(F32).sum(axis=0,keepdims=True)
    dbv_ref[...]+=df.astype(F32).sum(axis=0,keepdims=True)
    xh,rstd=row_stats(x_ref[...].astype(F32))
    db_ref[...]+=da.sum(axis=0,keepdims=True)
    dg_ref[...]+=(da*xh).sum(axis=0,keepdims=True)
    dxh=da*g_ref[...]
    gt_ref[...]=(dx_ref[...]+rstd*(dxh-jnp.mean(dxh,axis=-1,keepdims=True)-xh*jnp.mean(dxh*xh,axis=-1,keepdims=True))).astype(BF)

def last(dq,dk,df,w,x,dx,g,blk=256):
    rows,d=x.shape; vd=df.shape[1]
    rb=lambda n: pl.BlockSpec((blk,n),lambda i:(i,0))
    vec=lambda n: pl.BlockSpec((1,n),lambda i:(0,0))
    S=jax.ShapeDtypeStruct
    return pl.pallas_call(last_kernel,grid=(rows//blk,),
        in_specs=[rb(d),rb(d),rb(vd),full(w),rb(d),rb(d),full(g)],
        out_specs=[rb(d),vec(d),vec(d),vec(d),vec(vd)],
        out_shape=[S((rows,d),BF),S((1,d),F32),S((1,d),F32),S((1,d),F32),S((1,vd),F32)],
        compiler_params=pltpu.CompilerParams(vmem_limit_bytes=48<<20),
        cost_estimate=pl.CostEstimate(flops=2*rows*w.size,bytes_accessed=rows*d*14+2*w.size,transcendentals=0),
        name="input_grad")(dq,dk,df,w,x,dx,g)

AXES=("dp","fsdp")


def place(mesh):
    return mesh.shape["dp"], mesh.shape["fsdp"]//2

def shift_dp(v,k,zs):
    return lax.ppermute(v,"dp",[(i,(i+k)%zs) for i in range(zs)])

def swap_plane(v,k,planes):
    return lax.ppermute(v,"fsdp",[(i,i^(2*k)) for i in range(2*planes)])

def swap_core(v,planes):
    return lax.ppermute(v,"fsdp",[(i,i^1) for i in range(2*planes)])

def assemble_kernel(where_ref,*refs,planes,zs,piece):
    out=refs[-1]
    z=where_ref[0]; pn=where_ref[1]; core=where_ref[2]
    for p in range(planes):
        for k in range(zs):
            chip=lax.rem(z-k+zs,zs)*planes+jnp.bitwise_xor(pn,p)
            own=refs[p][k].astype(F32); sib=refs[planes+p][k].astype(F32)
            lo=jnp.where(core==0,own,sib); hi=jnp.where(core==0,sib,own)
            row=pl.multiple_of(chip*(2*piece),2*piece)
            out[pl.ds(row,2*piece),:]=jnp.concatenate([lo,hi],axis=0).astype(BF)

def assemble(where,pieces,planes,zs,name):
    _,piece,n=pieces[0].shape
    nblk=n//2 if (n//2)%128==0 else n
    if n%384==0: nblk=384
    return pl.pallas_call(functools.partial(assemble_kernel,planes=planes,zs=zs,piece=piece),grid=(n//nblk,),
        in_specs=[pl.BlockSpec(memory_space=pltpu.SMEM)]+[pl.BlockSpec((zs,piece,nblk),lambda i:(0,0,i))]*(2*planes),
        out_specs=pl.BlockSpec((2*planes*zs*piece,nblk),lambda i:(0,i)),
        out_shape=jax.ShapeDtypeStruct((2*planes*zs*piece,n),BF),
        compiler_params=pltpu.CompilerParams(vmem_limit_bytes=48<<20),
        cost_estimate=pl.CostEstimate(flops=0,bytes_accessed=8*planes*zs*piece*n,transcendentals=0),
        name=name)(where,*pieces)

def gather_pieces(w,zs,planes):
    mine=jnp.stack([w]+[shift_dp(w,k,zs) for k in range(1,zs)])
    own=[mine]+[swap_plane(mine,k,planes) for k in range(1,planes)]
    return own+[swap_core(t,planes) for t in own]

def scatter_sum(own,sib,zs,planes):
    got=swap_core(sib,planes)
    part=[(own[p].astype(F32)+got[p].astype(F32)).astype(BF) for p in range(planes)]
    total=part[0].astype(F32)
    for p in range(1,planes):
        total=total+swap_plane(part[p],p,planes).astype(F32)
    mine=total[0]
    rest=total.astype(BF)
    for k in range(1,zs):
        mine=mine+shift_dp(rest[k],k,zs).astype(F32)
    return mine

def swapped(v,flag,axis):
    return jnp.where(flag,jnp.flip(v,axis),v)

def gather_vectors(v,planes,plane,core):
    own=[v]+[swap_plane(v,k,planes) for k in range(1,planes)]
    own=jnp.stack(own)
    both=jnp.stack([own,swap_core(own,planes)],axis=1)
    both=swapped(both,core==1,1)
    bits=planes.bit_length()-1
    both=both.reshape((2,)*bits+both.shape[1:])
    for b in range(bits):
        both=swapped(both,((plane>>(bits-1-b))&1)==1,b)
    return both.reshape(-1)

def sum_vectors(v,zs,planes,plane,core):
    n=v.shape[0]//(2*planes)
    bits=planes.bit_length()-1
    v=v.reshape((2,)*(bits+1)+(n,))
    for b in range(bits):
        v=swapped(v,((plane>>(bits-1-b))&1)==1,b)
    v=swapped(v,core==1,bits)
    v=v.reshape(planes,2,n)
    part=v[:,0]+swap_core(v[:,1],planes)
    total=part[0]
    for p in range(1,planes):
        total=total+swap_plane(part[p],p,planes)
    mine=total
    for k in range(1,zs):
        mine=mine+shift_dp(total,k,zs)
    return mine

def local(zs,planes,tokens,first_values,cotangent,lengths,vectors,w_qkv,w_out,w_up,w_down):
    d=tokens.shape[1]; vd=first_values.shape[1]; ff=w_up.shape[1]
    fine=w_qkv.shape[0]%8==0 and w_down.shape[0]%8==0 and planes&(planes-1)==0
    index=lax.axis_index("fsdp")
    z=lax.axis_index("dp"); plane=index//2; core=index%2
    where=jnp.stack([z,plane,core]).astype(jnp.int32)
    def gather(w,name):
        if fine:
            return assemble(where,gather_pieces(w,zs,planes),planes,zs,name)
        return lax.all_gather(w,AXES,axis=0,tiled=True)
    def scatter(left,right,nblk,name):
        if fine:
            own,sib=weight_grad(where,left,right,planes,zs,nblk,name)
            return scatter_sum(own,sib,zs,planes)
        return lax.psum_scatter(lax.dot_general(left,right,(((0,),(0,)),((),())),preferred_element_type=F32),AXES,scatter_dimension=0,tiled=True)
    if fine: whole=gather_vectors(vectors,planes,plane,core)
    else: whole=lax.all_gather(vectors,"fsdp",axis=0,tiled=True)
    pieces=[]; at=0
    for n in (d,d,d,vd,d,d,d,ff,d):
        pieces.append(whole[at:at+n].reshape(1,n)); at+=n
    g1,b1,bq,bv,bo,g2,b2,bu,bd=pieces
    f_qkv=gather(w_qkv,"whole_qkv")
    f_down=gather(w_down,"whole_down")
    both=lax.all_gather(jnp.concatenate([w_up,w_out],axis=1),AXES,axis=0,tiled=True)
    f_up=both[:,:ff]; f_out=both[:,ff:]
    a1,q,k,v=project(tokens,first_values,g1,b1,bq,bv,f_qkv)
    o,lse=attend_forward(lengths,q,k,v)
    output,a2,y,du,dx1,dz,do,dbo,dg2,db2,dbu,dbd=mlp(o,tokens,cotangent,bo,g2,b2,bu,bd,f_out,f_up,f_down)
    grad_down=scatter(y,cotangent,768,"down_grad")
    grad_up=scatter(a2,du,1024,"up_grad")
    grad_out=scatter(o,dz,768,"out_grad")
    dq,dk,df,gf=attend_backward(lengths,q,k,v,o,do,lse)
    grad_qkv=scatter(a1,jnp.concatenate([dq,dk,df],axis=1),640,"qkv_grad")
    grad_tokens,dg1,db1,dbq,dbv=last(dq,dk,df,f_qkv,tokens,dx1,g1)
    vec=jnp.concatenate([t.reshape(-1) for t in (dg1,db1,dbq,dbv,dbo,dg2,db2,dbu,dbd)])
    if fine: grad_vectors=sum_vectors(vec,zs,planes,plane,core)
    else:
        n=vectors.shape[0]
        grad_vectors=lax.dynamic_slice_in_dim(lax.psum(vec,AXES),index*n,n,0)
    return output,grad_tokens,gf,grad_vectors,grad_qkv,grad_out,grad_up,grad_down

def solution(mesh):
    zs,planes=place(mesh)
    rows=P(AXES,None)
    return jax.shard_map(functools.partial(local,zs,planes),mesh=mesh,
        in_specs=(rows,rows,rows,rows,P("fsdp"),rows,rows,rows,rows),
        out_specs=(rows,rows,rows,P("fsdp"),rows,rows,rows,rows),check_vma=False)
```

time: 905 us -> 384 us (0.42)
  waiting for transfers between devices: 393 us -> 113 us
  matrix products: 267 us -> 0 us
  Pallas kernels: 0 us -> 148 us
  other arithmetic: 92.6 us -> 16.5 us
  starting transfers between devices: 0.32 us -> 67.3 us
  blocking collectives: 66.9 us -> 0 us
  local copies, waits for them, and re-layouts: 57 us -> 17.6 us
    reduce_scatter x3 -> x0, waiting for transfers between devices: 283 us -> none  [the longest x1 142 us: local(): lax.psum_scatter(grad_down, ('dp', 'fsdp'), scatter_dimension=0, tiled=True)]
    dot_general x26 -> x0, matrix products: 267 us -> none  [the longest x4 44.7 us: block_scores(): jnp.einsum('qhd,khd->hqk', part_query, keys, preferred_element_type=jnp.f...]
    pallas_call x0 -> x11, Pallas kernels: none -> 148 us  [the longest x1 35.9 us: mlp(): pl.pallas_call(mlp_kernel, grid=(rows // blk,), in_specs=[rb(d)] * 3 + [f...]
    ppermute x0 -> x59, waiting for transfers between devices: none -> 113 us  [the longest x24 96.6 us: swap_plane(): return lax.ppermute(v, 'fsdp', [(i, i ^ 2 * k) for i in range(2 * planes)])]
    all_gather x4 -> x1, waiting for transfers between devices: 101 us -> 0.01 us  [local(): lax.all_gather(jnp.concatenate([w_up, w_out], axis=1), AXES, axis=0, tile...]
    ppermute x0 -> x59, starting transfers between devices: none -> 67.2 us  [the longest x21 33.2 us: shift_dp(): return lax.ppermute(v, 'dp', [(i, (i + k) % zs) for i in range(zs)])]
    convert_element_type x6 -> x8, other arithmetic: 49.5 us -> 7.67 us  [the longest x4 4.39 us: scatter_sum(): (own[p].astype(F32) + got[p].astype(F32)).astype(BF)]
    psum x1 -> x0, blocking collectives: 40.8 us -> none  [local(): summed_vector = lax.psum(grad_vector, ('dp', 'fsdp'))]
  transfers between devices with their start and end apart: 8 -> 60, of which waited for: 6 -> 20; matrix products, arithmetic and copies ran while one was open for 40% -> 5% of each run, Pallas kernels for 0% -> 27%
where the time goes in v1:
time: 384 us; the launch traced here: 377 us
  Pallas kernels  148 us (39%)
  waiting for transfers between devices  113 us (29%)
  starting transfers between devices  67.3 us (18%)
  local copies, waits for them, and re-layouts  17.6 us (5%)
  other arithmetic  16.5 us (4%)
  between operations  15.1 us (4%)
    ppermute x24, waiting for transfers between devices, swap_plane(): return lax.ppermute(v, 'fsdp', [(i, i ^ 2 * k) for i in range(2 * planes)])  96.6 us
    pallas_call x1, Pallas kernels, mlp(): pl.pallas_call(mlp_kernel, grid=(rows // blk,), in_specs=[rb(d)] * 3 + [f...  35.9 us
    pallas_call x1, Pallas kernels, attend_backward(): pl.pallas_call(functools.partial(attend_backward_kernel, nfresh=nf), grid...  34.9 us
    ppermute x21, starting transfers between devices, shift_dp(): return lax.ppermute(v, 'dp', [(i, (i + k) % zs) for i in range(zs)])  33.2 us
    pallas_call x4, Pallas kernels, weight_grad(): pl.pallas_call(functools.partial(grad_kernel, planes=planes, zs=zs, piece...  32.9 us
    ppermute x24, starting transfers between devices, swap_plane(): return lax.ppermute(v, 'fsdp', [(i, i ^ 2 * k) for i in range(2 * planes)])  31.8 us
    pallas_call x1, Pallas kernels, attend_forward(): pl.pallas_call(attend_forward_kernel, grid=(n,), in_specs=[pl.BlockSpec(m...  20.7 us
    ppermute x21, waiting for transfers between devices, shift_dp(): return lax.ppermute(v, 'dp', [(i, (i + k) % zs) for i in range(zs)])  15.3 us
  transfers between devices with their start and end apart: 60, of which 20 were waited for; matrix products, arithmetic and copies ran while one was open for 5% of the time, Pallas kernels for 27%

profile of v1, /device:TPU:0, one launch (start us, length us, event | category | flops | bytes accessed | tf_op | source)
XLA Modules:
  0.0 377.4 jit_solution(16159988038708240100)
XLA Ops:
  7.2 1.6 pad_maximum_fusion.3
  8.9 3.0 collective-permute-start
  13.4 2.0 collective-permute-start.4
  15.5 2.6 collective-permute-start.5
  22.9 2.9 collective-permute-start.16
  28.0 2.2 collective-permute-start.7
  30.2 1.6 collective-permute-start.8
  31.8 7.1 %collective-permute-done.15 = bf16[96,768]{1,0:T(8,128)(2,1)S(1)} collective-permute-done((bf16[96,768]{1,0:T(8,128)(2,1)}, bf16[96,768]{1,0:T(8,128)(2,1)S(1)}, u32[]{:S(2)}, u32[]{:S(2)}) %collective-permute-start.15) | collective-permute-done | bytes 147488 | tf_op jit(solution)/shard_map/ppermute | solution.py:259
  39.0 1.6 collective-permute-start.17
  42.7 2.4 collective-permute-start.19
  45.1 24.6 %collective-permute-done.9.refs_3_ = bf16[4,24,1920]{2,1,0:T(8,128)(2,1)} collective-permute-done((bf16[4,24,1920]{2,1,0:T(8,128)(2,1)S(1)}, bf16[4,24,1920]{2,1,0:T(8,128)(2,1)}, u32[]{:S(2)}, u32[]{:S(2)}) %collective-permute-start.9) | collective-permute-done | bytes 368672 | tf_op jit(solution)/shard_map/ppermute | solution.py:262
  71.1 4.5 %collective-permute-done.18.refs_2_ = bf16[4,96,768]{2,1,0:T(8,128)(2,1)S(1)} collective-permute-done((bf16[4,96,768]{2,1,0:T(8,128)(2,1)S(1)}, bf16[4,96,768]{2,1,0:T(8,128)(2,1)S(1)}, u32[]{:S(2)}, u32[]{:S(2)}) %collective-permute-start.18) | collective-permute-done | bytes 589856 | tf_op jit(solution)/shard_map/ppermute | solution.py:262
  75.6 15.2 %collective-permute-done.19.refs_3_ = bf16[4,96,768]{2,1,0:T(8,128)(2,1)S(1)} collective-permute-done((bf16[4,96,768]{2,1,0:T(8,128)(2,1)S(1)}, bf16[4,96,768]{2,1,0:T(8,128)(2,1)S(1)}, u32[]{:S(2)}, u32[]{:S(2)}) %collective-permute-start.19) | collective-permute-done | bytes 589856 | tf_op jit(solution)/shard_map/ppermute | solution.py:262
  95.3 3.8 %whole_qkv.1.w_ref = bf16[768,1920]{1,0:T(8,128)(2,1)S(1)} custom-call(s32[3]{0:T(128)S(1)} %pad_add_fusion.where_ref, bf16[4,24,1920]{2,1,0:T(8,128)(2,1)S(1)} %pad_maximum_fusion.2.refs_0_, bf16[4,24,1920]{2,1,0:T(8,128)(2,1)S(1)} %collective-permute-done.7.refs_1_, bf16[4,24,1920]{2,1,0:T(8,128)(2,1)S(1)} %collective-permute-done.8.refs_2_, ...), custom_call_target="tpu_custom_call" | custom-call | bytes 5898240 | tf_op jit(solution)/shard_map/whole_qkv/pallas_call | solution.py:282
  99.1 1.6 copy-done
  100.7 8.0 %project.1 = (bf16[1024,768]{1,0:T(8,128)(2,1)S(1)}, bf16[1024,768]{1,0:T(8,128)(2,1)S(1)}, bf16[1024,768]{1,0:T(8,128)(2,1)S(1)}, bf16[1024,768]{1,0:T(8,128)(2,1)}) custom-call(bf16[1024,768]{1,0:T(8,128)(2,1)} %x_ref.5, bf16[1024,384]{1,0:T(8,128)(2,1)S(1)} %copy-done.5, f32[1,768]{1,0:T(1,128)S(1)} %reshape.156.g_ref, f32[1,768]{1,0:T(1,128)S(1)} %reshape.157.b_ref, ...), custom_call_target="tpu_custom_call" | custom-call | flops 3019898880 | bytes 10813440 | tf_op jit(solution)/shard_map/project/pallas_call | solution.py:134
  109.9 20.7 %attend_forward.1 = (bf16[1024,768]{1,0:T(8,128)(2,1)S(1)}, f32[6,2,1024]{2,1,0:T(2,128)S(1)}) custom-call(s32[1,2]{1,0:T(1,128)S(1)} %copy-done.6, bf16[1024,768]{1,0:T(8,128)(2,1)S(1)} %get-tuple-element.43.q_ref, bf16[1024,768]{1,0:T(8,128)(2,1)S(1)} %get-tuple-element.44.k_ref, bf16[1024,768]{1,0:T(8,128)(2,1)} %get-tuple-element.45.v_ref), custom_call_target="tpu_custom_call" | custom-call | flops 3221225472 | bytes 6291456 | tf_op jit(solution)/shard_map/attend_forward/pallas_call | solution.py:47
  131.8 3.6 whole_down.1.wd_ref
  135.4 4.8 %slice.270.wu_ref = bf16[768,3072]{1,0:T(8,128)(2,1)} slice(bf16[768,3840]{1,0:T(8,128)(2,1)} %all-gather.2.cloned.1.call-done), slice={[0:768], [0:3072]} | slice | bytes 9437184 | tf_op jit(solution)/shard_map/slice | solution.py:362
  140.1 2.4 slice.269.wo_ref
  142.5 35.9 %feed_forward.1 = (bf16[1024,768]{1,0:T(8,128)(2,1)}, bf16[1024,768]{1,0:T(8,128)(2,1)}, bf16[1024,3072]{1,0:T(8,128)(2,1)}, bf16[1024,3072]{1,0:T(8,128)(2,1)},...) custom-call(bf16[1024,768]{1,0:T(8,128)(2,1)} %copy-done.7, ...), custom_call_target="tpu_custom_call" | custom-call | flops 21743271936 | bytes 37355520 | tf_op jit(solution)/shard_map/feed_forward/pallas_call | solution.py:189
  178.4 10.6 %down_grad.1 = (bf16[4,4,96,768]{3,2,1,0:T(8,128)(2,1)}, bf16[4,4,96,768]{3,2,1,0:T(8,128)(2,1)}) custom-call(s32[3]{0:T(128)} %copy-done.4, bf16[1024,3072]{1,0:T(8,128)(2,1)} %get-tuple-element.75.l_ref, bf16[1024,768]{1,0:T(8,128)(2,1)} %r_ref.1), custom_call_target="tpu_custom_call" | custom-call | flops 4831838208 | bytes 12582912 | tf_op jit(solution)/shard_map/down_grad/pallas_call | solution.py:216
  189.3 4.5 %out_grad.1 = (bf16[4,4,24,768]{3,2,1,0:T(8,128)(2,1)}, bf16[4,4,24,768]{3,2,1,0:T(8,128)(2,1)}) custom-call(s32[3]{0:T(128)} %copy-done.4, bf16[1024,768]{1,0:T(8,128)(2,1)} %copy-done.7, bf16[1024,768]{1,0:T(8,128)(2,1)} %get-tuple-element.68.r_ref), custom_call_target="tpu_custom_call" | custom-call | flops 1207959552 | bytes 4325376 | tf_op jit(solution)/shard_map/out_grad/pallas_call | solution.py:216
  194.0 34.9 %attend_backward.1 = (bf16[1024,768]{1,0:T(8,128)(2,1)S(1)}, bf16[1024,768]{1,0:T(8,128)(2,1)S(1)}, bf16[1024,384]{1,0:T(8,128)(2,1)S(1)}, bf16[1024,384]{1,0:T(8,128)(2,1)}) custom-call(s32[1,2]{1,0:T(1,128)S(1)} %copy-done.6, bf16[1024,768]{1,0:T(8,128)(2,1)S(1)} %copy-done.10, bf16[1024,768]{1,0:T(8,128)(2,1)} %copy-done.11, ...), custom_call_target="tpu_custom_call" | custom-call | flops 8053063680 | bytes 12582912 | tf_op jit(solution)/shard_map/attend_backward/pallas_call | solution.py:103
  229.0 2.2 pad_maximum_fusion.r_ref
  231.1 8.2 %qkv_grad.1 = (bf16[4,4,24,1920]{3,2,1,0:T(8,128)(2,1)}, bf16[4,4,24,1920]{3,2,1,0:T(8,128)(2,1)}) custom-call(s32[3]{0:T(128)} %copy-done.4, bf16[1024,768]{1,0:T(8,128)(2,1)} %copy-done.8, bf16[1024,1920]{1,0:T(8,128)(2,1)} %pad_maximum_fusion.r_ref), custom_call_target="tpu_custom_call" | custom-call | flops 3019898880 | bytes 8454144 | tf_op jit(solution)/shard_map/qkv_grad/pallas_call | solution.py:216
  239.6 8.2 %input_grad.1 = (bf16[1024,768]{1,0:T(8,128)(2,1)}, f32[1,768]{1,0:T(1,128)S(1)}, f32[1,768]{1,0:T(1,128)S(1)}, f32[1,768]{1,0:T(1,128)S(1)}, f32[1,384]{1,0:T(1,128)S(1)}) custom-call(bf16[1024,768]{1,0:T(8,128)(2,1)S(1)} %get-tuple-element.50.dq_ref, bf16[1024,768]{1,0:T(8,128)(2,1)S(1)} %get-tuple-element.51.dk_ref, ...), custom_call_target="tpu_custom_call" | custom-call | flops 3019898880 | bytes 13959168 | tf_op jit(solution)/shard_map/input_grad/pallas_call | solution.py:244
  249.0 9.6 %up_grad.1 = (bf16[4,4,24,3072]{3,2,1,0:T(8,128)(2,1)}, bf16[4,4,24,3072]{3,2,1,0:T(8,128)(2,1)}) custom-call(s32[3]{0:T(128)} %copy-done.4, bf16[1024,768]{1,0:T(8,128)(2,1)} %get-tuple-element.71.l_ref, bf16[1024,3072]{1,0:T(8,128)(2,1)} %get-tuple-element.72.r_ref), custom_call_target="tpu_custom_call" | custom-call | flops 4831838208 | bytes 12582912 | tf_op jit(solution)/shard_map/up_grad/pallas_call | solution.py:216
  260.7 1.6 collective-permute-start.27
  265.2 1.7 collective-permute-start.41
  268.0 4.0 %collective-permute-done.40 = bf16[4,24,768]{2,1,0:T(8,128)(2,1)S(1)} collective-permute-done((bf16[4,24,768]{2,1,0:T(8,128)(2,1)S(1)}, bf16[4,24,768]{2,1,0:T(8,128)(2,1)S(1)}, u32[]{:S(2)}, u32[]{:S(2)}) %collective-permute-start.40) | collective-permute-done | bytes 147488 | tf_op jit(solution)/shard_map/ppermute | solution.py:262
  272.0 4.7 %collective-permute-start.28 = (f32[1104]{0:T(1024)S(1)}, f32[1104]{0:T(1024)S(1)}, u32[]{:S(2)}, u32[]{:S(2)}) collective-permute-start(f32[1104]{0:T(1024)S(1)} %add_add_fusion.1), channel_id=1, source_target_pairs={{0,8},{8,16},{16,24},{24,0},{1,9},{9,17},{17,25},{25,1},{2,10},{10... | collective-permute-start | bytes 13256 | tf_op jit(solution)/shard_map/ppermute | solution.py:259
  278.3 2.0 collective-permute-start.30
  283.6 2.8 collective-permute-start.44
  288.9 2.6 collective-permute-start.34
  292.8 3.9 %collective-permute-done.32 = bf16[4,24,1920]{2,1,0:T(8,128)(2,1)S(1)} collective-permute-done((bf16[4,24,1920]{2,1,0:T(8,128)(2,1)S(1)}, bf16[4,24,1920]{2,1,0:T(8,128)(2,1)S(1)}, u32[]{:S(2)}, u32[]{:S(2)}) %collective-permute-start.32) | collective-permute-done | bytes 368672 | tf_op jit(solution)/shard_map/ppermute | solution.py:262
  296.7 5.5 %collective-permute-done.33 = bf16[4,24,1920]{2,1,0:T(8,128)(2,1)S(1)} collective-permute-done((bf16[4,24,1920]{2,1,0:T(8,128)(2,1)S(1)}, bf16[4,24,1920]{2,1,0:T(8,128)(2,1)S(1)}, u32[]{:S(2)}, u32[]{:S(2)}) %collective-permute-start.33) | collective-permute-done | bytes 368672 | tf_op jit(solution)/shard_map/ppermute | solution.py:262
  305.4 2.7 collective-permute-start.37
  308.1 2.1 fusion.11
  310.2 2.0 collective-permute-start.53
  314.5 2.0 collective-permute-start.46
  316.6 10.0 %collective-permute-done.53 = bf16[4,96,768]{2,1,0:T(8,128)(2,1)S(1)} collective-permute-done((bf16[4,96,768]{2,1,0:T(8,128)(2,1)S(1)}, bf16[4,96,768]{2,1,0:T(8,128)(2,1)S(1)}, u32[]{:S(2)}, u32[]{:S(2)}) %collective-permute-start.53) | collective-permute-done | bytes 589856 | tf_op jit(solution)/shard_map/ppermute | solution.py:262
  328.3 12.8 %collective-permute-done.54 = bf16[4,96,768]{2,1,0:T(8,128)(2,1)S(1)} collective-permute-done((bf16[4,96,768]{2,1,0:T(8,128)(2,1)S(1)}, bf16[4,96,768]{2,1,0:T(8,128)(2,1)S(1)}, u32[]{:S(2)}, u32[]{:S(2)}) %collective-permute-start.54) | collective-permute-done | bytes 589856 | tf_op jit(solution)/shard_map/ppermute | solution.py:262
  344.3 7.1 %collective-permute-done.46 = bf16[4,24,3072]{2,1,0:T(8,128)(2,1)S(1)} collective-permute-done((bf16[4,24,3072]{2,1,0:T(8,128)(2,1)S(1)}, bf16[4,24,3072]{2,1,0:T(8,128)(2,1)S(1)}, u32[]{:S(2)}, u32[]{:S(2)}) %collective-permute-start.46) | collective-permute-done | bytes 589856 | tf_op jit(solution)/shard_map/ppermute | solution.py:262
  352.2 6.9 %collective-permute-done.47 = bf16[4,24,3072]{2,1,0:T(8,128)(2,1)S(1)} collective-permute-done((bf16[4,24,3072]{2,1,0:T(8,128)(2,1)S(1)}, bf16[4,24,3072]{2,1,0:T(8,128)(2,1)S(1)}, u32[]{:S(2)}, u32[]{:S(2)}) %collective-permute-start.47) | collective-permute-done | bytes 589856 | tf_op jit(solution)/shard_map/ppermute | solution.py:262
  361.4 2.8 collective-permute-start.51
  365.0 1.8 collective-permute-done.49
  366.8 2.5 collective-permute-done.50
  (206 shorter events, 50.5 us)
Async XLA Ops:
  7.2 128.2 %all-gather.2.cloned.1.call-start = ((), (), s32[]{:S(2)}) async-start(), calls=%async_computation | async-start | bytes 6082560 | tf_op jit(solution)/shard_map/all_gather | solution.py:361
  8.9 9.9 %collective-permute-start = (f32[1104]{0:T(1024)}, f32[1104]{0:T(1024)S(1)}, u32[]{:S(2)}, u32[]{:S(2)}) collective-permute-start(f32[1104]{0:T(1024)} %param.13), channel_id=1, source_target_pairs={{0,2},{1,3},{2,0},{3,1},{4,6},{5,7},{6,4},{7,5},{8,10},{9,11},{10,... | collective-permute-start | bytes 13256 | tf_op jit(solution)/shard_map/ppermute | solution.py:262
  11.9 8.2 %collective-permute-start.1 = (f32[1104]{0:T(1024)}, f32[1104]{0:T(1024)S(1)}, u32[]{:S(2)}, u32[]{:S(2)}) collective-permute-start(f32[1104]{0:T(1024)} %param.13), channel_id=1, source_target_pairs={{0,4},{1,5},{2,6},{3,7},{4,0},{5,1},{6,2},{7,3},{8,12},{9,13},{10,... | collective-permute-start | bytes 13256 | tf_op jit(solution)/shard_map/ppermute | solution.py:262
  13.4 7.4 %collective-permute-start.2 = (f32[1104]{0:T(1024)}, f32[1104]{0:T(1024)S(1)}, u32[]{:S(2)}, u32[]{:S(2)}) collective-permute-start(f32[1104]{0:T(1024)} %param.13), channel_id=1, source_target_pairs={{0,6},{1,7},{2,4},{3,5},{4,2},{5,3},{6,0},{7,1},{8,14},{9,15},{10,... | collective-permute-start | bytes 13256 | tf_op jit(solution)/shard_map/ppermute | solution.py:262
  13.4 9.4 %collective-permute-start.4 = (bf16[24,1920]{1,0:T(8,128)(2,1)}, bf16[24,1920]{1,0:T(8,128)(2,1)S(1)}, u32[]{:S(2)}, u32[]{:S(2)}) collective-permute-start(bf16[24,1920]{1,0:T(8,128)(2,1)} %param.14), channel_id=1, source_target_pairs={{0,8},{8,16},{16,24},{24,0},{1,9},{9,17},{17,25},{25,1},{2,10},{10... | collective-permute-start | bytes 276488 | tf_op jit(solution)/shard_map/ppermute | solution.py:259
  15.5 10.3 %collective-permute-start.5 = (bf16[24,1920]{1,0:T(8,128)(2,1)}, bf16[24,1920]{1,0:T(8,128)(2,1)S(1)}, u32[]{:S(2)}, u32[]{:S(2)}) collective-permute-start(bf16[24,1920]{1,0:T(8,128)(2,1)} %param.14), channel_id=1, source_target_pairs={{0,16},{8,24},{16,0},{24,8},{1,17},{9,25},{17,1},{25,9},{2,18},{10... | collective-permute-start | bytes 276488 | tf_op jit(solution)/shard_map/ppermute | solution.py:259
  18.8 8.3 %collective-permute-start.6 = (bf16[24,1920]{1,0:T(8,128)(2,1)}, bf16[24,1920]{1,0:T(8,128)(2,1)S(1)}, u32[]{:S(2)}, u32[]{:S(2)}) collective-permute-start(bf16[24,1920]{1,0:T(8,128)(2,1)} %param.14), channel_id=1, source_target_pairs={{0,24},{8,0},{16,8},{24,16},{1,25},{9,1},{17,9},{25,17},{2,26},{10... | collective-permute-start | bytes 276488 | tf_op jit(solution)/shard_map/ppermute | solution.py:259
  20.1 11.7 %collective-permute-start.14 = (bf16[96,768]{1,0:T(8,128)(2,1)}, bf16[96,768]{1,0:T(8,128)(2,1)S(1)}, u32[]{:S(2)}, u32[]{:S(2)}) collective-permute-start(bf16[96,768]{1,0:T(8,128)(2,1)} %param.17), channel_id=1, source_target_pairs={{0,8},{8,16},{16,24},{24,0},{1,9},{9,17},{17,25},{25,1},{2,10},{10... | collective-permute-start | bytes 442376 | tf_op jit(solution)/shard_map/ppermute | solution.py:259
  22.2 16.7 %collective-permute-start.15 = (bf16[96,768]{1,0:T(8,128)(2,1)}, bf16[96,768]{1,0:T(8,128)(2,1)S(1)}, u32[]{:S(2)}, u32[]{:S(2)}) collective-permute-start(bf16[96,768]{1,0:T(8,128)(2,1)} %param.17), channel_id=1, source_target_pairs={{0,16},{8,24},{16,0},{24,8},{1,17},{9,25},{17,1},{25,9},{2,18},{10... | collective-permute-start | bytes 442376 | tf_op jit(solution)/shard_map/ppermute | solution.py:259
  22.9 16.0 %collective-permute-start.16 = (bf16[96,768]{1,0:T(8,128)(2,1)}, bf16[96,768]{1,0:T(8,128)(2,1)S(1)}, u32[]{:S(2)}, u32[]{:S(2)}) collective-permute-start(bf16[96,768]{1,0:T(8,128)(2,1)} %param.17), channel_id=1, source_target_pairs={{0,24},{8,0},{16,8},{24,16},{1,25},{9,1},{17,9},{25,17},{2,26},{10... | collective-permute-start | bytes 442376 | tf_op jit(solution)/shard_map/ppermute | solution.py:259
  28.0 14.2 %collective-permute-start.7 = (bf16[4,24,1920]{2,1,0:T(8,128)(2,1)S(1)}, bf16[4,24,1920]{2,1,0:T(8,128)(2,1)S(1)}, u32[]{:S(2)}, u32[]{:S(2)}) collective-permute-start(bf16[4,24,1920]{2,1,0:T(8,128)(2,1)S(1)} %pad_maximum_fusion.2.refs_0_), channel_id=1, source_target_pairs={{0,2},{1,3},{2,0},{3,1},{4,6},{5,7},{6,4},{7,5},{8,10},{9,11},{10,... | collective-permute-start | bytes 1105928 | tf_op jit(solution)/shard_map/ppermute | solution.py:262
  30.2 12.5 %collective-permute-start.8 = (bf16[4,24,1920]{2,1,0:T(8,128)(2,1)S(1)}, bf16[4,24,1920]{2,1,0:T(8,128)(2,1)S(1)}, u32[]{:S(2)}, u32[]{:S(2)}) collective-permute-start(bf16[4,24,1920]{2,1,0:T(8,128)(2,1)S(1)} %pad_maximum_fusion.2.refs_0_), channel_id=1, source_target_pairs={{0,4},{1,5},{2,6},{3,7},{4,0},{5,1},{6,2},{7,3},{8,12},{9,13},{10,... | collective-permute-start | bytes 1105928 | tf_op jit(solution)/shard_map/ppermute | solution.py:262
  39.0 32.0 %collective-permute-start.17 = (bf16[4,96,768]{2,1,0:T(8,128)(2,1)S(1)}, bf16[4,96,768]{2,1,0:T(8,128)(2,1)S(1)}, u32[]{:S(2)}, u32[]{:S(2)}) collective-permute-start(bf16[4,96,768]{2,1,0:T(8,128)(2,1)S(1)} %pad_maximum_fusion.1.refs_0_), channel_id=1, source_target_pairs={{0,2},{1,3},{2,0},{3,1},{4,6},{5,7},{6,4},{7,5},{8,10},{9,11},{10,... | collective-permute-start | bytes 1769480 | tf_op jit(solution)/shard_map/ppermute | solution.py:262
  40.6 29.1 %collective-permute-start.9 = (bf16[4,24,1920]{2,1,0:T(8,128)(2,1)S(1)}, bf16[4,24,1920]{2,1,0:T(8,128)(2,1)}, u32[]{:S(2)}, u32[]{:S(2)}) collective-permute-start(bf16[4,24,1920]{2,1,0:T(8,128)(2,1)S(1)} %pad_maximum_fusion.2.refs_0_), channel_id=1, source_target_pairs={{0,6},{1,7},{2,4},{3,5},{4,2},{5,3},{6,0},{7,1},{8,14},{9,15},{10,... | collective-permute-start | bytes 1105928 | tf_op jit(solution)/shard_map/ppermute | solution.py:262
  42.2 27.5 %collective-permute-start.10 = (bf16[4,24,1920]{2,1,0:T(8,128)(2,1)S(1)}, bf16[4,24,1920]{2,1,0:T(8,128)(2,1)S(1)}, u32[]{:S(2)}, u32[]{:S(2)}) collective-permute-start(bf16[4,24,1920]{2,1,0:T(8,128)(2,1)S(1)} %pad_maximum_fusion.2.refs_0_), channel_id=1, source_target_pairs={{0,1},{1,0},{2,3},{3,2},{4,5},{5,4},{6,7},{7,6},{8,9},{9,8},{10,11... | collective-permute-start | bytes 1105928 | tf_op jit(solution)/shard_map/ppermute | solution.py:265
  42.2 33.4 %collective-permute-start.18 = (bf16[4,96,768]{2,1,0:T(8,128)(2,1)S(1)}, bf16[4,96,768]{2,1,0:T(8,128)(2,1)S(1)}, u32[]{:S(2)}, u32[]{:S(2)}) collective-permute-start(bf16[4,96,768]{2,1,0:T(8,128)(2,1)S(1)} %pad_maximum_fusion.1.refs_0_), channel_id=1, source_target_pairs={{0,4},{1,5},{2,6},{3,7},{4,0},{5,1},{6,2},{7,3},{8,12},{9,13},{10,... | collective-permute-start | bytes 1769480 | tf_op jit(solution)/shard_map/ppermute | solution.py:262
  42.7 48.1 %collective-permute-start.19 = (bf16[4,96,768]{2,1,0:T(8,128)(2,1)S(1)}, bf16[4,96,768]{2,1,0:T(8,128)(2,1)S(1)}, u32[]{:S(2)}, u32[]{:S(2)}) collective-permute-start(bf16[4,96,768]{2,1,0:T(8,128)(2,1)S(1)} %pad_maximum_fusion.1.refs_0_), channel_id=1, source_target_pairs={{0,6},{1,7},{2,4},{3,5},{4,2},{5,3},{6,0},{7,1},{8,14},{9,15},{10,... | collective-permute-start | bytes 1769480 | tf_op jit(solution)/shard_map/ppermute | solution.py:262
  69.7 21.1 %collective-permute-start.11 = (bf16[4,24,1920]{2,1,0:T(8,128)(2,1)S(1)}, bf16[4,24,1920]{2,1,0:T(8,128)(2,1)}, u32[]{:S(2)}, u32[]{:S(2)}) collective-permute-start(bf16[4,24,1920]{2,1,0:T(8,128)(2,1)S(1)} %collective-permute-done.7.refs_1_), channel_id=1, source_target_pairs={{0,1},{1,0},{2,3},{3,2},{4,5},{5,4},{6,7},{7,6},{8,9},{9,8},{10,11... | collective-permute-start | bytes 1105928 | tf_op jit(solution)/shard_map/ppermute | solution.py:265
  70.4 20.8 %collective-permute-start.12 = (bf16[4,24,1920]{2,1,0:T(8,128)(2,1)S(1)}, bf16[4,24,1920]{2,1,0:T(8,128)(2,1)}, u32[]{:S(2)}, u32[]{:S(2)}) collective-permute-start(bf16[4,24,1920]{2,1,0:T(8,128)(2,1)S(1)} %collective-permute-done.8.refs_2_), channel_id=1, source_target_pairs={{0,1},{1,0},{2,3},{3,2},{4,5},{5,4},{6,7},{7,6},{8,9},{9,8},{10,11... | collective-permute-start | bytes 1105928 | tf_op jit(solution)/shard_map/ppermute | solution.py:265
  71.0 23.4 %collective-permute-start.13 = (bf16[4,24,1920]{2,1,0:T(8,128)(2,1)}, bf16[4,24,1920]{2,1,0:T(8,128)(2,1)}, u32[]{:S(2)}, u32[]{:S(2)}) collective-permute-start(bf16[4,24,1920]{2,1,0:T(8,128)(2,1)} %collective-permute-done.9.refs_3_), channel_id=1, source_target_pairs={{0,1},{1,0},{2,3},{3,2},{4,5},{5,4},{6,7},{7,6},{8,9},{9,8},{10,11... | collective-permute-start | bytes 1105928 | tf_op jit(solution)/shard_map/ppermute | solution.py:265
  75.6 56.2 %collective-permute-start.20 = (bf16[4,96,768]{2,1,0:T(8,128)(2,1)S(1)}, bf16[4,96,768]{2,1,0:T(8,128)(2,1)S(1)}, u32[]{:S(2)}, u32[]{:S(2)}) collective-permute-start(bf16[4,96,768]{2,1,0:T(8,128)(2,1)S(1)} %pad_maximum_fusion.1.refs_0_), channel_id=1, source_target_pairs={{0,1},{1,0},{2,3},{3,2},{4,5},{5,4},{6,7},{7,6},{8,9},{9,8},{10,11... | collective-permute-start | bytes 1769480 | tf_op jit(solution)/shard_map/ppermute | solution.py:265
  90.8 41.0 %collective-permute-start.21 = (bf16[4,96,768]{2,1,0:T(8,128)(2,1)S(1)}, bf16[4,96,768]{2,1,0:T(8,128)(2,1)S(1)}, u32[]{:S(2)}, u32[]{:S(2)}) collective-permute-start(bf16[4,96,768]{2,1,0:T(8,128)(2,1)S(1)} %collective-permute-done.17.refs_1_), channel_id=1, source_target_pairs={{0,1},{1,0},{2,3},{3,2},{4,5},{5,4},{6,7},{7,6},{8,9},{9,8},{10,11... | collective-permute-start | bytes 1769480 | tf_op jit(solution)/shard_map/ppermute | solution.py:265
  90.8 41.0 %collective-permute-start.22 = (bf16[4,96,768]{2,1,0:T(8,128)(2,1)S(1)}, bf16[4,96,768]{2,1,0:T(8,128)(2,1)S(1)}, u32[]{:S(2)}, u32[]{:S(2)}) collective-permute-start(bf16[4,96,768]{2,1,0:T(8,128)(2,1)S(1)} %collective-permute-done.18.refs_2_), channel_id=1, source_target_pairs={{0,1},{1,0},{2,3},{3,2},{4,5},{5,4},{6,7},{7,6},{8,9},{9,8},{10,11... | collective-permute-start | bytes 1769480 | tf_op jit(solution)/shard_map/ppermute | solution.py:265
  91.3 40.5 %collective-permute-start.23 = (bf16[4,96,768]{2,1,0:T(8,128)(2,1)S(1)}, bf16[4,96,768]{2,1,0:T(8,128)(2,1)S(1)}, u32[]{:S(2)}, u32[]{:S(2)}) collective-permute-start(bf16[4,96,768]{2,1,0:T(8,128)(2,1)S(1)} %collective-permute-done.19.refs_3_), channel_id=1, source_target_pairs={{0,1},{1,0},{2,3},{3,2},{4,5},{5,4},{6,7},{7,6},{8,9},{9,8},{10,11... | collective-permute-start | bytes 1769480 | tf_op jit(solution)/shard_map/ppermute | solution.py:265
  189.0 119.1 %collective-permute-start.52 = (bf16[4,4,96,768]{3,2,1,0:T(8,128)(2,1)}, bf16[4,4,96,768]{3,2,1,0:T(8,128)(2,1)}, u32[]{:S(2)}, u32[]{:S(2)}) collective-permute-start(bf16[4,4,96,768]{3,2,1,0:T(8,128)(2,1)} %get-tuple-element.77), channel_id=1, source_target_pairs={{0,1},{1,0},{2,3},{3,2},{4,5},{5,4},{6,7},{7,6},{8,9},{9,8},{10,11... | collective-permute-start | bytes 7077896 | tf_op jit(solution)/shard_map/ppermute | solution.py:265
  193.8 66.8 %collective-permute-start.38 = (bf16[4,4,24,768]{3,2,1,0:T(8,128)(2,1)}, bf16[4,4,24,768]{3,2,1,0:T(8,128)(2,1)S(1)}, u32[]{:S(2)}, u32[]{:S(2)}) collective-permute-start(bf16[4,4,24,768]{3,2,1,0:T(8,128)(2,1)} %get-tuple-element.70), channel_id=1, source_target_pairs={{0,1},{1,0},{2,3},{3,2},{4,5},{5,4},{6,7},{7,6},{8,9},{9,8},{10,11... | collective-permute-start | bytes 1769480 | tf_op jit(solution)/shard_map/ppermute | solution.py:265
  239.3 44.3 %collective-permute-start.31 = (bf16[4,4,24,1920]{3,2,1,0:T(8,128)(2,1)}, bf16[4,4,24,1920]{3,2,1,0:T(8,128)(2,1)}, u32[]{:S(2)}, u32[]{:S(2)}) collective-permute-start(bf16[4,4,24,1920]{3,2,1,0:T(8,128)(2,1)} %get-tuple-element.67), channel_id=1, source_target_pairs={{0,1},{1,0},{2,3},{3,2},{4,5},{5,4},{6,7},{7,6},{8,9},{9,8},{10,11... | collective-permute-start | bytes 4423688 | tf_op jit(solution)/shard_map/ppermute | solution.py:265
  248.7 9.9 %collective-permute-start.24 = (f32[4,1104]{1,0:T(4,128)S(1)}, f32[4,1104]{1,0:T(4,128)S(1)}, u32[]{:S(2)}, u32[]{:S(2)}) collective-permute-start(f32[4,1104]{1,0:T(4,128)S(1)} %bitcast.138), channel_id=1, source_target_pairs={{0,1},{1,0},{2,3},{3,2},{4,5},{5,4},{6,7},{7,6},{8,9},{9,8},{10,11... | collective-permute-start | bytes 53000 | tf_op jit(solution)/shard_map/ppermute | solution.py:265
  263.7 8.3 %collective-permute-start.40 = (bf16[4,24,768]{2,1,0:T(8,128)(2,1)S(1)}, bf16[4,24,768]{2,1,0:T(8,128)(2,1)S(1)}, u32[]{:S(2)}, u32[]{:S(2)}) collective-permute-start(bf16[4,24,768]{2,1,0:T(8,128)(2,1)S(1)} %get-tuple-element.101), channel_id=1, source_target_pairs={{0,4},{1,5},{2,6},{3,7},{4,0},{5,1},{6,2},{7,3},{8,12},{9,13},{10,... | collective-permute-start | bytes 442376 | tf_op jit(solution)/shard_map/ppermute | solution.py:262
  265.2 11.5 %collective-permute-start.41 = (bf16[4,24,768]{2,1,0:T(8,128)(2,1)S(1)}, bf16[4,24,768]{2,1,0:T(8,128)(2,1)S(1)}, u32[]{:S(2)}, u32[]{:S(2)}) collective-permute-start(bf16[4,24,768]{2,1,0:T(8,128)(2,1)S(1)} %get-tuple-element.100), channel_id=1, source_target_pairs={{0,6},{1,7},{2,4},{3,5},{4,2},{5,3},{6,0},{7,1},{8,14},{9,15},{10,... | collective-permute-start | bytes 442376 | tf_op jit(solution)/shard_map/ppermute | solution.py:262
  268.0 44.3 %collective-permute-start.45 = (bf16[4,4,24,3072]{3,2,1,0:T(8,128)(2,1)}, bf16[4,4,24,3072]{3,2,1,0:T(8,128)(2,1)S(1)}, u32[]{:S(2)}, u32[]{:S(2)}) collective-permute-start(bf16[4,4,24,3072]{3,2,1,0:T(8,128)(2,1)} %get-tuple-element.74), channel_id=1, source_target_pairs={{0,1},{1,0},{2,3},{3,2},{4,5},{5,4},{6,7},{7,6},{8,9},{9,8},{10,11... | collective-permute-start | bytes 7077896 | tf_op jit(solution)/shard_map/ppermute | solution.py:265
  287.9 8.7 %collective-permute-start.32 = (bf16[4,24,1920]{2,1,0:T(8,128)(2,1)S(1)}, bf16[4,24,1920]{2,1,0:T(8,128)(2,1)S(1)}, u32[]{:S(2)}, u32[]{:S(2)}) collective-permute-start(bf16[4,24,1920]{2,1,0:T(8,128)(2,1)S(1)} %get-tuple-element.96), channel_id=1, source_target_pairs={{0,2},{1,3},{2,0},{3,1},{4,6},{5,7},{6,4},{7,5},{8,10},{9,11},{10,... | collective-permute-start | bytes 1105928 | tf_op jit(solution)/shard_map/ppermute | solution.py:262
  288.9 13.3 %collective-permute-start.33 = (bf16[4,24,1920]{2,1,0:T(8,128)(2,1)S(1)}, bf16[4,24,1920]{2,1,0:T(8,128)(2,1)S(1)}, u32[]{:S(2)}, u32[]{:S(2)}) collective-permute-start(bf16[4,24,1920]{2,1,0:T(8,128)(2,1)S(1)} %get-tuple-element.98), channel_id=1, source_target_pairs={{0,4},{1,5},{2,6},{3,7},{4,0},{5,1},{6,2},{7,3},{8,12},{9,13},{10,... | collective-permute-start | bytes 1105928 | tf_op jit(solution)/shard_map/ppermute | solution.py:262
  288.9 13.3 %collective-permute-start.34 = (bf16[4,24,1920]{2,1,0:T(8,128)(2,1)S(1)}, bf16[4,24,1920]{2,1,0:T(8,128)(2,1)S(1)}, u32[]{:S(2)}, u32[]{:S(2)}) collective-permute-start(bf16[4,24,1920]{2,1,0:T(8,128)(2,1)S(1)} %get-tuple-element.97), channel_id=1, source_target_pairs={{0,6},{1,7},{2,4},{3,5},{4,2},{5,3},{6,0},{7,1},{8,14},{9,15},{10,... | collective-permute-start | bytes 1105928 | tf_op jit(solution)/shard_map/ppermute | solution.py:262
  303.4 8.8 %collective-permute-start.35 = (bf16[24,1920]{1,0:T(8,128)(2,1)S(1)}, bf16[24,1920]{1,0:T(8,128)(2,1)S(1)}, u32[]{:S(2)}, u32[]{:S(2)}) collective-permute-start(bf16[24,1920]{1,0:T(8,128)(2,1)S(1)} %get-tuple-element.108), channel_id=1, source_target_pairs={{0,8},{8,16},{16,24},{24,0},{1,9},{9,17},{17,25},{25,1},{2,10},{10... | collective-permute-start | bytes 276488 | tf_op jit(solution)/shard_map/ppermute | solution.py:259
  304.1 10.3 %collective-permute-start.36 = (bf16[24,1920]{1,0:T(8,128)(2,1)S(1)}, bf16[24,1920]{1,0:T(8,128)(2,1)S(1)}, u32[]{:S(2)}, u32[]{:S(2)}) collective-permute-start(bf16[24,1920]{1,0:T(8,128)(2,1)S(1)} %get-tuple-element.110), channel_id=1, source_target_pairs={{0,16},{8,24},{16,0},{24,8},{1,17},{9,25},{17,1},{25,9},{2,18},{10... | collective-permute-start | bytes 276488 | tf_op jit(solution)/shard_map/ppermute | solution.py:259
  305.4 11.1 %collective-permute-start.37 = (bf16[24,1920]{1,0:T(8,128)(2,1)S(1)}, bf16[24,1920]{1,0:T(8,128)(2,1)S(1)}, u32[]{:S(2)}, u32[]{:S(2)}) collective-permute-start(bf16[24,1920]{1,0:T(8,128)(2,1)S(1)} %get-tuple-element.109), channel_id=1, source_target_pairs={{0,24},{8,0},{16,8},{24,16},{1,25},{9,1},{17,9},{25,17},{2,26},{10... | collective-permute-start | bytes 276488 | tf_op jit(solution)/shard_map/ppermute | solution.py:259
  310.2 16.3 %collective-permute-start.53 = (bf16[4,96,768]{2,1,0:T(8,128)(2,1)S(1)}, bf16[4,96,768]{2,1,0:T(8,128)(2,1)S(1)}, u32[]{:S(2)}, u32[]{:S(2)}) collective-permute-start(bf16[4,96,768]{2,1,0:T(8,128)(2,1)S(1)} %get-tuple-element.90), channel_id=1, source_target_pairs={{0,2},{1,3},{2,0},{3,1},{4,6},{5,7},{6,4},{7,5},{8,10},{9,11},{10,... | collective-permute-start | bytes 1769480 | tf_op jit(solution)/shard_map/ppermute | solution.py:262
  312.3 28.9 %collective-permute-start.54 = (bf16[4,96,768]{2,1,0:T(8,128)(2,1)S(1)}, bf16[4,96,768]{2,1,0:T(8,128)(2,1)S(1)}, u32[]{:S(2)}, u32[]{:S(2)}) collective-permute-start(bf16[4,96,768]{2,1,0:T(8,128)(2,1)S(1)} %get-tuple-element.92), channel_id=1, source_target_pairs={{0,4},{1,5},{2,6},{3,7},{4,0},{5,1},{6,2},{7,3},{8,12},{9,13},{10,... | collective-permute-start | bytes 1769480 | tf_op jit(solution)/shard_map/ppermute | solution.py:262
  312.3 28.9 %collective-permute-start.55 = (bf16[4,96,768]{2,1,0:T(8,128)(2,1)S(1)}, bf16[4,96,768]{2,1,0:T(8,128)(2,1)S(1)}, u32[]{:S(2)}, u32[]{:S(2)}) collective-permute-start(bf16[4,96,768]{2,1,0:T(8,128)(2,1)S(1)} %get-tuple-element.91), channel_id=1, source_target_pairs={{0,6},{1,7},{2,4},{3,5},{4,2},{5,3},{6,0},{7,1},{8,14},{9,15},{10,... | collective-permute-start | bytes 1769480 | tf_op jit(solution)/shard_map/ppermute | solution.py:262
  314.5 36.9 %collective-permute-start.46 = (bf16[4,24,3072]{2,1,0:T(8,128)(2,1)S(1)}, bf16[4,24,3072]{2,1,0:T(8,128)(2,1)S(1)}, u32[]{:S(2)}, u32[]{:S(2)}) collective-permute-start(bf16[4,24,3072]{2,1,0:T(8,128)(2,1)S(1)} %get-tuple-element.93), channel_id=1, source_target_pairs={{0,2},{1,3},{2,0},{3,1},{4,6},{5,7},{6,4},{7,5},{8,10},{9,11},{10,... | collective-permute-start | bytes 1769480 | tf_op jit(solution)/shard_map/ppermute | solution.py:262
  316.5 42.6 %collective-permute-start.47 = (bf16[4,24,3072]{2,1,0:T(8,128)(2,1)S(1)}, bf16[4,24,3072]{2,1,0:T(8,128)(2,1)S(1)}, u32[]{:S(2)}, u32[]{:S(2)}) collective-permute-start(bf16[4,24,3072]{2,1,0:T(8,128)(2,1)S(1)} %get-tuple-element.95), channel_id=1, source_target_pairs={{0,4},{1,5},{2,6},{3,7},{4,0},{5,1},{6,2},{7,3},{8,12},{9,13},{10,... | collective-permute-start | bytes 1769480 | tf_op jit(solution)/shard_map/ppermute | solution.py:262
  326.6 32.5 %collective-permute-start.48 = (bf16[4,24,3072]{2,1,0:T(8,128)(2,1)S(1)}, bf16[4,24,3072]{2,1,0:T(8,128)(2,1)S(1)}, u32[]{:S(2)}, u32[]{:S(2)}) collective-permute-start(bf16[4,24,3072]{2,1,0:T(8,128)(2,1)S(1)} %get-tuple-element.94), channel_id=1, source_target_pairs={{0,6},{1,7},{2,4},{3,5},{4,2},{5,3},{6,0},{7,1},{8,14},{9,15},{10,... | collective-permute-start | bytes 1769480 | tf_op jit(solution)/shard_map/ppermute | solution.py:262
  342.7 18.7 %collective-permute-start.56 = (bf16[96,768]{1,0:T(8,128)(2,1)S(1)}, bf16[96,768]{1,0:T(8,128)(2,1)S(1)}, u32[]{:S(2)}, u32[]{:S(2)}) collective-permute-start(bf16[96,768]{1,0:T(8,128)(2,1)S(1)} %get-tuple-element.102), channel_id=1, source_target_pairs={{0,8},{8,16},{16,24},{24,0},{1,9},{9,17},{17,25},{25,1},{2,10},{10... | collective-permute-start | bytes 442376 | tf_op jit(solution)/shard_map/ppermute | solution.py:259
  342.8 21.4 %collective-permute-start.57 = (bf16[96,768]{1,0:T(8,128)(2,1)S(1)}, bf16[96,768]{1,0:T(8,128)(2,1)S(1)}, u32[]{:S(2)}, u32[]{:S(2)}) collective-permute-start(bf16[96,768]{1,0:T(8,128)(2,1)S(1)} %get-tuple-element.104), channel_id=1, source_target_pairs={{0,16},{8,24},{16,0},{24,8},{1,17},{9,25},{17,1},{25,9},{2,18},{10... | collective-permute-start | bytes 442376 | tf_op jit(solution)/shard_map/ppermute | solution.py:259
  351.4 12.9 %collective-permute-start.58 = (bf16[96,768]{1,0:T(8,128)(2,1)S(1)}, bf16[96,768]{1,0:T(8,128)(2,1)S(1)}, u32[]{:S(2)}, u32[]{:S(2)}) collective-permute-start(bf16[96,768]{1,0:T(8,128)(2,1)S(1)} %get-tuple-element.103), channel_id=1, source_target_pairs={{0,24},{8,0},{16,8},{24,16},{1,25},{9,1},{17,9},{25,17},{2,26},{10... | collective-permute-start | bytes 442376 | tf_op jit(solution)/shard_map/ppermute | solution.py:259
  360.1 9.2 %collective-permute-start.50 = (bf16[24,3072]{1,0:T(8,128)(2,1)S(1)}, bf16[24,3072]{1,0:T(8,128)(2,1)S(1)}, u32[]{:S(2)}, u32[]{:S(2)}) collective-permute-start(bf16[24,3072]{1,0:T(8,128)(2,1)S(1)} %get-tuple-element.107), channel_id=1, source_target_pairs={{0,16},{8,24},{16,0},{24,8},{1,17},{9,25},{17,1},{25,9},{2,18},{10... | collective-permute-start | bytes 442376 | tf_op jit(solution)/shard_map/ppermute | solution.py:259
  361.4 8.0 %collective-permute-start.51 = (bf16[24,3072]{1,0:T(8,128)(2,1)S(1)}, bf16[24,3072]{1,0:T(8,128)(2,1)S(1)}, u32[]{:S(2)}, u32[]{:S(2)}) collective-permute-start(bf16[24,3072]{1,0:T(8,128)(2,1)S(1)} %get-tuple-element.106), channel_id=1, source_target_pairs={{0,24},{8,0},{16,8},{24,16},{1,25},{9,1},{17,9},{25,17},{2,26},{10... | collective-permute-start | bytes 442376 | tf_op jit(solution)/shard_map/ppermute | solution.py:259
  (35 other events, 389.0 us)
Sparse Core Ops, SparseCore 0:
  11.5 91.2 all-gather.1
